TPU v7x, 32 devices: a whole 2x2x4 slice. The times are simulated.
32 devices in a mesh: dp: 4 (over z), seq: 8 (over y, x, core).
Axes of the slice: x: 2, y: 2, z: 4, core: 2. Of those that a mesh axis runs over, the one named last changes fastest.
Arguments:
- tokens: bfloat16 [8, 4096, 768], P('dp', 'seq'), may hold values from -6 to 6
- w_qkv: bfloat16 [768, 2304], P(('dp', 'seq')), may hold values from -0.21875 to 0.21875
- qv_bias: bfloat16 [1536], P(('dp', 'seq')), may hold values from -1.1953125 to 1.1953125
- w_proj: bfloat16 [768, 768], P(('dp', 'seq')), may hold values from -3 to 3
- proj_bias: bfloat16 [768], P(('dp', 'seq')), may hold values from -1.1953125 to 1.1953125
- w_fc1: bfloat16 [768, 3072], P(('dp', 'seq')), may hold values from -0.21875 to 0.21875
- fc1_bias: bfloat16 [3072], P(('dp', 'seq')), may hold values from -1.1953125 to 1.1953125
- w_fc2: bfloat16 [3072, 768], P(('dp', 'seq')), may hold values from -0.15625 to 0.15625
- fc2_bias: bfloat16 [768], P(('dp', 'seq')), may hold values from -1.1953125 to 1.1953125
- norm_gains: bfloat16 [2, 768], P(None, ('dp', 'seq')), may hold values from 0.5 to 1.5
- norm_biases: bfloat16 [2, 768], P(None, ('dp', 'seq')), may hold values from -1.1953125 to 1.1953125
- rel_tables: bfloat16 [2, 127, 64], replicated, may hold values from -0.75 to 0.75
- cotangent: bfloat16 [8, 4096, 768], P('dp', 'seq'), may hold values from -6 to 6
Outputs:
- result: bfloat16 [8, 4096, 768], P('dp', 'seq')
- tokens_grad: bfloat16 [8, 4096, 768], P('dp', 'seq')
- w_qkv_grad: float32 [768, 2304], P(('dp', 'seq'))
- qv_bias_grad: float32 [1536], P(('dp', 'seq'))
- w_proj_grad: float32 [768, 768], P(('dp', 'seq'))
- proj_bias_grad: float32 [768], P(('dp', 'seq'))
- w_fc1_grad: float32 [768, 3072], P(('dp', 'seq'))
- fc1_bias_grad: float32 [3072], P(('dp', 'seq'))
- w_fc2_grad: float32 [3072, 768], P(('dp', 'seq'))
- fc2_bias_grad: float32 [768], P(('dp', 'seq'))
- norm_gains_grad: float32 [2, 768], P(None, ('dp', 'seq'))
- norm_biases_grad: float32 [2, 768], P(None, ('dp', 'seq'))
- rel_tables_grad: float32 [2, 127, 64], replicated
All inputs are finite; a program needn't handle non-finite values.
Results may differ from a plain program's by a relative error of at most 0.013.
Values may be sent and summed in bfloat16 or wider, within the bound.
No kernel may reach another device: no remote copies, remote signals or barrier semaphores. Data moves between devices by JAX's collectives and lax.ppermute only.
A program may use at most 832 MiB of HBM per device.

v0:
```python
from functools import partial

import jax
import jax.numpy as jnp
from jax import lax
from jax.sharding import PartitionSpec as P

HEADS = 12
HD = 64
GRID = 64
MB = 2
TABLE = 127


EPS = 1e-06
HIGH = lax.Precision.HIGHEST


def layer_norm(values, gain, shift):
    center = jnp.mean(values, axis=-1, keepdims=True)
    centered = values - center
    spread = jnp.mean(centered * centered, axis=-1, keepdims=True)
    return centered * lax.rsqrt(spread + EPS) * gain + shift


def fetch_each(weights):
    return (
        lax.all_gather(weights[0], ("dp", "seq"), axis=0, tiled=True),
        lax.all_gather(weights[1], ("dp", "seq"), axis=0, tiled=True),
        lax.all_gather(weights[2], ("dp", "seq"), axis=0, tiled=True),
        lax.all_gather(weights[3], ("dp", "seq"), axis=0, tiled=True),
        lax.all_gather(weights[4], ("dp", "seq"), axis=0, tiled=True),
        lax.all_gather(weights[5], ("dp", "seq"), axis=0, tiled=True),
        lax.all_gather(weights[6], ("dp", "seq"), axis=0, tiled=True),
        lax.all_gather(weights[7], ("dp", "seq"), axis=0, tiled=True),
        lax.all_gather(weights[8], ("dp", "seq"), axis=1, tiled=True),
        lax.all_gather(weights[9], ("dp", "seq"), axis=1, tiled=True),
    )


def position_rows(tables, rows_img):
    beginning = lax.axis_index("seq") * rows_img
    tokens_at = beginning + jnp.arange(rows_img, dtype=jnp.int32)
    offsets = jnp.arange(GRID, dtype=jnp.int32)
    entries = jnp.arange(TABLE, dtype=jnp.int32)
    row_index = tokens_at[:, None] // GRID - offsets[None, :] + GRID - 1
    col_index = tokens_at[:, None] % GRID - offsets[None, :] + GRID - 1
    row_hot = (row_index[:, :, None] == entries[None, None, :]).astype(jnp.float32)
    col_hot = (col_index[:, :, None] == entries[None, None, :]).astype(jnp.float32)
    tables_f = tables.astype(jnp.float32)
    rel_rows = jnp.einsum("rkt,tc->rkc", row_hot, tables_f[0], precision=HIGH)
    rel_cols = jnp.einsum("rkt,tc->rkc", col_hot, tables_f[1], precision=HIGH)
    return (row_hot, col_hot, rel_rows, rel_cols)


def score_block(queries, keys_all, rows_low, cols_low):
    rows_img = queries.shape[0]
    product = jnp.einsum(
        "rhc,nhc->hrn", queries, keys_all, preferred_element_type=jnp.float32
    ) * HD ** (-0.5)
    bias_rows = jnp.einsum("rhc,rkc->hrk", queries, rows_low, preferred_element_type=jnp.float32)
    bias_cols = jnp.einsum("rhc,rkc->hrk", queries, cols_low, preferred_element_type=jnp.float32)
    joined = (
        product.reshape(HEADS, rows_img, GRID, GRID)
        + bias_rows[:, :, :, None]
        + bias_cols[:, :, None, :]
    )
    return joined.reshape(HEADS, rows_img, GRID * GRID)


def attend_forward(qkv_img, kv_pair, rows_low, cols_low):
    rows_img, triple = qkv_img.shape
    features = triple // 3
    queries = qkv_img[:, :features].reshape(rows_img, HEADS, HD)
    keys_all = kv_pair[0].reshape(-1, HEADS, HD)
    values_all = kv_pair[1].reshape(-1, HEADS, HD)
    scores = score_block(queries, keys_all, rows_low, cols_low)
    largest = jnp.max(scores, axis=-1, keepdims=True)
    shifted = jnp.exp(scores - largest)
    totals = jnp.sum(shifted, axis=-1, keepdims=True)
    probs_low = (shifted / totals).astype(jnp.bfloat16)
    attended = jnp.einsum("hrn,nhc->rhc", probs_low, values_all, preferred_element_type=jnp.float32)
    log_totals = largest[..., 0] + jnp.log(totals[..., 0])
    return (attended.reshape(rows_img, features).astype(jnp.bfloat16), log_totals)


def attend_backward(qkv_img, log_totals, grad_att, kv_pair, rel_rows, rel_cols, rows_low, cols_low):
    rows_img, triple = qkv_img.shape
    features = triple // 3
    scale = HD ** (-0.5)
    queries = qkv_img[:, :features].reshape(rows_img, HEADS, HD)
    keys_all = kv_pair[0].reshape(-1, HEADS, HD)
    values_all = kv_pair[1].reshape(-1, HEADS, HD)
    scores = score_block(queries, keys_all, rows_low, cols_low)
    probs = jnp.exp(scores - log_totals[..., None])
    probs_low = probs.astype(jnp.bfloat16)
    grad_heads = grad_att.reshape(rows_img, HEADS, HD)
    grad_probs = jnp.einsum(
        "rhc,nhc->hrn", grad_heads, values_all, preferred_element_type=jnp.float32
    )
    inner_sum = jnp.sum(probs * grad_probs, axis=-1, keepdims=True)
    grad_scores = (probs * (grad_probs - inner_sum)).astype(jnp.bfloat16)
    grad_queries = (
        jnp.einsum("hrn,nhc->rhc", grad_scores, keys_all, preferred_element_type=jnp.float32)
        * scale
    )
    grid_scores = grad_scores.reshape(HEADS, rows_img, GRID, GRID)
    grad_rows = jnp.sum(grid_scores, axis=3, dtype=jnp.float32)
    grad_cols = jnp.sum(grid_scores, axis=2, dtype=jnp.float32)
    grad_queries = grad_queries + jnp.einsum("hrk,rkc->rhc", grad_rows, rel_rows, precision=HIGH)
    grad_queries = grad_queries + jnp.einsum("hrk,rkc->rhc", grad_cols, rel_cols, precision=HIGH)
    query_f = queries.astype(jnp.float32)
    table_rows = jnp.einsum("hrk,rhc->rkc", grad_rows, query_f, precision=HIGH)
    table_cols = jnp.einsum("hrk,rhc->rkc", grad_cols, query_f, precision=HIGH)
    length = lax.axis_size("seq") * rows_img
    grad_keys = (
        jnp.einsum("hrn,rhc->nhc", grad_scores, queries, preferred_element_type=jnp.float32) * scale
    )
    grad_values = jnp.einsum(
        "hrn,rhc->nhc", probs_low, grad_heads, preferred_element_type=jnp.float32
    )
    key_grads = lax.psum_scatter(
        jnp.concatenate(
            [grad_keys.reshape(length, features), grad_values.reshape(length, features)], axis=1
        ),
        "seq",
        scatter_dimension=0,
        tiled=True,
    )
    grad_qkv = jnp.concatenate(
        [grad_queries.reshape(rows_img, features), key_grads], axis=1
    ).astype(jnp.bfloat16)
    return (grad_qkv, table_rows, table_cols)


def body(
    tokens,
    w_qkv,
    qv_bias,
    w_proj,
    proj_bias,
    w_fc1,
    fc1_bias,
    w_fc2,
    fc2_bias,
    norm_gains,
    norm_biases,
    rel_tables,
    cotangent,
):
    images, rows_img, features = tokens.shape
    per_batch = images // MB
    weights = (
        w_qkv,
        qv_bias,
        w_proj,
        proj_bias,
        w_fc1,
        fc1_bias,
        w_fc2,
        fc2_bias,
        norm_gains,
        norm_biases,
    )
    row_hot, col_hot, rel_rows, rel_cols = position_rows(rel_tables, rows_img)
    rows_low = rel_rows.astype(jnp.bfloat16)
    cols_low = rel_cols.astype(jnp.bfloat16)
    stored = []
    outputs = []
    for batch_index in range(MB):
        gathered = fetch_each(weights)
        (
            wq_full,
            bqv_full,
            wp_full,
            bp_full,
            w1_full,
            b1_full,
            w2_full,
            b2_full,
            gains_full,
            shifts_full,
        ) = gathered
        gains_f = gains_full.astype(jnp.float32)
        shifts_f = shifts_full.astype(jnp.float32)
        inputs = (
            tokens[batch_index * per_batch : (batch_index + 1) * per_batch]
            .astype(jnp.float32)
            .reshape(-1, features)
        )
        normed1 = layer_norm(inputs, gains_f[0], shifts_f[0]).astype(jnp.bfloat16)
        full_bias = jnp.concatenate(
            [bqv_full[:features], jnp.zeros((features,), bqv_full.dtype), bqv_full[features:]]
        ).astype(jnp.float32)
        qkv = (jnp.dot(normed1, wq_full, preferred_element_type=jnp.float32) + full_bias).astype(
            jnp.bfloat16
        )
        qkv_images = qkv.reshape(per_batch, rows_img, 3 * features)

        def forward_image(carried, qkv_img):
            kv_pair = (
                lax.all_gather(qkv_img[:, features : 2 * features], "seq", axis=0, tiled=True),
                lax.all_gather(qkv_img[:, 2 * features :], "seq", axis=0, tiled=True),
            )
            attended_img, log_totals = attend_forward(qkv_img, kv_pair, rows_low, cols_low)
            return (carried, (attended_img, log_totals))

        results = lax.scan(forward_image, jnp.zeros((), jnp.float32), qkv_images)[1]
        attended = results[0].reshape(-1, features)
        mixed = (
            inputs
            + jnp.dot(attended, wp_full, preferred_element_type=jnp.float32)
            + bp_full.astype(jnp.float32)
        )
        normed2 = layer_norm(mixed, gains_f[1], shifts_f[1]).astype(jnp.bfloat16)
        pre = jnp.dot(normed2, w1_full, preferred_element_type=jnp.float32) + b1_full.astype(
            jnp.float32
        )
        activated = jax.nn.gelu(pre, approximate=False).astype(jnp.bfloat16)
        block_out = (
            mixed
            + jnp.dot(activated, w2_full, preferred_element_type=jnp.float32)
            + b2_full.astype(jnp.float32)
        )
        outputs.append(block_out.astype(jnp.bfloat16).reshape(per_batch, rows_img, features))
        stored.append((normed1, qkv_images, results, mixed, normed2, pre, activated))
    gradients = [jnp.zeros(array.shape, jnp.float32) for array in gathered]
    table_rows_sum = jnp.zeros((rows_img, GRID, HD), jnp.float32)
    table_cols_sum = jnp.zeros((rows_img, GRID, HD), jnp.float32)
    input_grads = []
    for batch_index in range(MB):
        gathered = fetch_each(weights)
        (
            wq_full,
            bqv_full,
            wp_full,
            bp_full,
            w1_full,
            b1_full,
            w2_full,
            b2_full,
            gains_full,
            shifts_full,
        ) = gathered
        gains_f = gains_full.astype(jnp.float32)
        shifts_f = shifts_full.astype(jnp.float32)
        normed1, qkv_images, results, mixed, normed2, pre, activated = stored[batch_index]
        inputs = (
            tokens[batch_index * per_batch : (batch_index + 1) * per_batch]
            .astype(jnp.float32)
            .reshape(-1, features)
        )
        grad_out = cotangent[batch_index * per_batch : (batch_index + 1) * per_batch].reshape(
            -1, features
        )
        grad_out_f = grad_out.astype(jnp.float32)
        grad_w2 = jnp.dot(activated.T, grad_out, preferred_element_type=jnp.float32)
        grad_b2 = jnp.sum(grad_out_f, axis=0)
        grad_act = jnp.dot(grad_out, w2_full.T, preferred_element_type=jnp.float32)
        _, gelu_pull = jax.vjp(partial(jax.nn.gelu, approximate=False), pre)
        grad_pre = gelu_pull(grad_act)[0].astype(jnp.bfloat16)
        grad_w1 = jnp.dot(normed2.T, grad_pre, preferred_element_type=jnp.float32)
        grad_b1 = jnp.sum(grad_pre, axis=0, dtype=jnp.float32)
        grad_norm2 = jnp.dot(grad_pre, w1_full.T, preferred_element_type=jnp.float32)
        _, norm_pull2 = jax.vjp(layer_norm, mixed, gains_f[1], shifts_f[1])
        grad_mix_norm, grad_gain2, grad_shift2 = norm_pull2(grad_norm2)
        grad_mixed = grad_out_f + grad_mix_norm
        grad_branch = grad_mixed.astype(jnp.bfloat16)
        attended = results[0].reshape(-1, features)
        grad_wp = jnp.dot(attended.T, grad_branch, preferred_element_type=jnp.float32)
        grad_bp = jnp.sum(grad_branch, axis=0, dtype=jnp.float32)
        grad_att = jnp.dot(grad_branch, wp_full.T, preferred_element_type=jnp.float32).astype(
            jnp.bfloat16
        )
        grad_images = grad_att.reshape(per_batch, rows_img, features)
        image_inputs = (qkv_images, results[1], grad_images)

        def backward_image(carried, pieces):
            kv_pair = (
                lax.all_gather(pieces[0][:, features : 2 * features], "seq", axis=0, tiled=True),
                lax.all_gather(pieces[0][:, 2 * features :], "seq", axis=0, tiled=True),
            )
            grad_qkv_img, table_rows, table_cols = attend_backward(
                pieces[0], pieces[1], pieces[2], kv_pair, rel_rows, rel_cols, rows_low, cols_low
            )
            return ((carried[0] + table_rows, carried[1] + table_cols), grad_qkv_img)

        (table_rows_sum, table_cols_sum), grad_qkv_all = lax.scan(
            backward_image, (table_rows_sum, table_cols_sum), image_inputs
        )
        grad_qkv = grad_qkv_all.reshape(-1, 3 * features)
        grad_wq = jnp.dot(normed1.T, grad_qkv, preferred_element_type=jnp.float32)
        grad_bqv = jnp.concatenate(
            [
                jnp.sum(grad_qkv[:, :features], axis=0, dtype=jnp.float32),
                jnp.sum(grad_qkv[:, 2 * features :], axis=0, dtype=jnp.float32),
            ]
        )
        grad_norm1 = jnp.dot(grad_qkv, wq_full.T, preferred_element_type=jnp.float32)
        _, norm_pull1 = jax.vjp(layer_norm, inputs, gains_f[0], shifts_f[0])
        grad_in_norm, grad_gain1, grad_shift1 = norm_pull1(grad_norm1)
        input_grads.append(
            (grad_mixed + grad_in_norm).astype(jnp.bfloat16).reshape(per_batch, rows_img, features)
        )
        updates = (
            grad_wq,
            grad_bqv,
            grad_wp,
            grad_bp,
            grad_w1,
            grad_b1,
            grad_w2,
            grad_b2,
            jnp.stack([grad_gain1, grad_gain2]),
            jnp.stack([grad_shift1, grad_shift2]),
        )
        gradients = [before + update for before, update in zip(gradients, updates)]
    summed = (
        lax.psum_scatter(gradients[0], ("dp", "seq"), scatter_dimension=0, tiled=True),
        lax.psum_scatter(gradients[1], ("dp", "seq"), scatter_dimension=0, tiled=True),
        lax.psum_scatter(gradients[2], ("dp", "seq"), scatter_dimension=0, tiled=True),
        lax.psum_scatter(gradients[3], ("dp", "seq"), scatter_dimension=0, tiled=True),
        lax.psum_scatter(gradients[4], ("dp", "seq"), scatter_dimension=0, tiled=True),
        lax.psum_scatter(gradients[5], ("dp", "seq"), scatter_dimension=0, tiled=True),
        lax.psum_scatter(gradients[6], ("dp", "seq"), scatter_dimension=0, tiled=True),
        lax.psum_scatter(gradients[7], ("dp", "seq"), scatter_dimension=0, tiled=True),
        lax.psum_scatter(gradients[8], ("dp", "seq"), scatter_dimension=1, tiled=True),
        lax.psum_scatter(gradients[9], ("dp", "seq"), scatter_dimension=1, tiled=True),
    )
    table_local = jnp.stack(
        [
            jnp.einsum("rkt,rkc->tc", row_hot, table_rows_sum, precision=HIGH),
            jnp.einsum("rkt,rkc->tc", col_hot, table_cols_sum, precision=HIGH),
        ]
    )
    table_grad = lax.psum(table_local, ("dp", "seq"))
    return (
        jnp.concatenate(outputs, axis=0),
        jnp.concatenate(input_grads, axis=0),
        summed[0],
        summed[1],
        summed[2],
        summed[3],
        summed[4],
        summed[5],
        summed[6],
        summed[7],
        summed[8],
        summed[9],
        table_grad,
    )


def solution(mesh):
    placed = (
        P("dp", "seq", None),
        P(("dp", "seq"), None),
        P(("dp", "seq")),
        P(("dp", "seq"), None),
        P(("dp", "seq")),
        P(("dp", "seq"), None),
        P(("dp", "seq")),
        P(("dp", "seq"), None),
        P(("dp", "seq")),
        P(None, ("dp", "seq")),
        P(None, ("dp", "seq")),
        P(),
        P("dp", "seq", None),
    )
    return jax.shard_map(
        body,
        mesh=mesh,
        in_specs=placed,
        out_specs=(
            P("dp", "seq", None),
            P("dp", "seq", None),
            P(("dp", "seq"), None),
            P(("dp", "seq")),
            P(("dp", "seq"), None),
            P(("dp", "seq")),
            P(("dp", "seq"), None),
            P(("dp", "seq")),
            P(("dp", "seq"), None),
            P(("dp", "seq")),
            P(None, ("dp", "seq")),
            P(None, ("dp", "seq")),
            P(),
        ),
        check_vma=False,
    )
```

profile of v0, /device:TPU:0, one launch (start us, length us, event | category | flops | bytes accessed | tf_op | source)
XLA Modules:
  0.0 2938.5 jit_solution(13776367262540203346)
XLA Ops:
  8.0 43.3 %all-gather.1 = bf16[32,24,2]{1,2,0:T(2,128)(2,1)S(1)} all-gather(bf16[1,24,2]{1,2,0:T(2,128)(2,1)} %bitcast.310), channel_id=1, replica_groups=mesh['dp'=4,'seq'=8] {'dp','seq'}, dimensions={0}, use_global_device_ids=true | all-gather | bytes 3168 | tf_op jit(solution)/shard_map/all_gather | solution.py:37
  51.6 36.8 %all-gather = bf16[32,24,2]{1,2,0:T(2,128)(2,1)S(1)} all-gather(bf16[1,24,2]{1,2,0:T(2,128)(2,1)} %bitcast.311), channel_id=1, replica_groups=mesh['dp'=4,'seq'=8] {'dp','seq'}, dimensions={0}, use_global_device_ids=true | all-gather | bytes 3168 | tf_op jit(solution)/shard_map/all_gather | solution.py:36
  92.0 37.1 %all-reduce.11 = (bf16[1536]{0:T(1024)(128)(2,1)S(1)}, bf16[768]{0:T(1024)(128)(2,1)S(1)}, bf16[3072]{0:T(1024)(128)(2,1)S(1)}, bf16[768]{0:T(1024)(128)(2,1)}) all-reduce(bf16[1536]{0:T(1024)(128)(2,1)S(1)} %dynamic-update-slice, bf16[768]{0:T(1024)(128)(2,1)S(1)} %dynamic-update-slice.1, ...), channel_id=1, replica_groups=mesh['dp'=4,'seq'=8] {'dp','seq'}, use_global_device_ids=true, to_apply=%add | all-reduce | flops 6144 | bytes 24576
  246.1 31.5 %add.429 = f32[12,512,64,64]{1,3,2,0:T(8,128)} broadcast(f32[12,512,64]{1,2,0:T(8,128)S(1)} %copy.168), dimensions={0,1,3} | broadcast | bytes 102236160 | tf_op jit(solution)/shard_map/while/body/eval_jaxpr/add | solution.py:64
  277.6 99.2 %copy.169 = f32[12,512,4096]{2,1,0:T(8,128)} copy(f32[12,512,4096]{1,2,0:T(8,128)} %bitcast.28) | data formatting | bytes 201326592 | tf_op jit(solution)/shard_map/while/body/eval_jaxpr/add | solution.py:64
  379.8 31.5 %add.426 = f32[12,512,64,64]{1,3,2,0:T(8,128)} broadcast(f32[12,512,64]{1,2,0:T(8,128)S(1)} %copy.164), dimensions={0,1,2} | broadcast | bytes 102236160 | tf_op jit(solution)/shard_map/while/body/eval_jaxpr/add | solution.py:64
  411.3 99.0 %copy.165 = f32[12,512,4096]{2,1,0:T(8,128)} copy(f32[12,512,4096]{1,2,0:T(8,128)} %bitcast.26) | data formatting | bytes 201326592 | tf_op jit(solution)/shard_map/while/body/eval_jaxpr/add | solution.py:64
  513.4 31.4 %add.408 = f32[12,512,64,64]{1,3,2,0:T(8,128)} broadcast(f32[12,512,64]{1,2,0:T(8,128)S(1)} %copy.157), dimensions={0,1,3} | broadcast | bytes 102236160 | tf_op jit(solution)/shard_map/while/body/eval_jaxpr/add | solution.py:64
  544.8 98.6 %copy.158 = f32[12,512,4096]{2,1,0:T(8,128)} copy(f32[12,512,4096]{1,2,0:T(8,128)} %bitcast.17) | data formatting | bytes 201326592 | tf_op jit(solution)/shard_map/while/body/eval_jaxpr/add | solution.py:64
  646.5 31.5 %add.404 = f32[12,512,64,64]{1,3,2,0:T(8,128)} broadcast(f32[12,512,64]{1,2,0:T(8,128)S(1)} %copy.153), dimensions={0,1,2} | broadcast | bytes 102236160 | tf_op jit(solution)/shard_map/while/body/eval_jaxpr/add | solution.py:64
  678.0 98.6 %copy.154 = f32[12,512,4096]{2,1,0:T(8,128)} copy(f32[12,512,4096]{1,2,0:T(8,128)} %bitcast.13) | data formatting | bytes 201326592 | tf_op jit(solution)/shard_map/while/body/eval_jaxpr/add | solution.py:64
  785.3 98.6 %fusion.135 = (f32[12,512]{1,0:T(8,128)S(1)}, f32[12,512,4096]{2,1,0:T(8,128)}) fusion(f32[12,512,4096]{2,1,0:T(8,128)} %copy.169, f32[12,512,4096]{2,1,0:T(8,128)} %copy.165, bf16[512,12,64]{0,2,1:T(8,128)(2,1)S(1)} %bitcast.291, bf16[4096,12,64]{0,2,1:T(8,128)(2,1)} %bitcast.278), kind=kOutput, calls=%fused_computation.249 | convolution fusion | flops 3321882624 | bytes 309092352 | tf_op jit(solution)/shard_map/while/body/eval_jaxpr/rhc,nhc->hrn/dot_general | solution.py:58
  884.0 31.0 %fusion.1 = f32[12,512]{1,0:T(8,128)S(1)} fusion(f32[12,512,4096]{2,1,0:T(8,128)} %get-tuple-element.190, f32[12,512]{1,0:T(8,128)S(1)} %get-tuple-element.189), kind=kLoop, calls=%fused_computation.13 | loop fusion | flops 50325504 | bytes 100712448 | tf_op jit(solution)/shard_map/while/body/eval_jaxpr/reduce_sum | solution.py:80
  923.7 35.3 %fusion.71 = bf16[12,64,512]{2,1,0:T(8,128)(2,1)S(1)} fusion(bf16[4096,12,64]{0,2,1:T(8,128)(2,1)} %bitcast.286, f32[12,512,4096]{2,1,0:T(8,128)} %get-tuple-element.190, f32[12,512]{1,0:T(8,128)S(1)} %fusion.1, f32[12,512]{1,0:T(8,128)S(1)} %get-tuple-element.189), kind=kOutput, calls=%fused_computation.161 | convolution fusion | flops 3297116160 | bytes 107790336 | tf_op jit(solution)/shard_map/while/body/eval_jaxpr/hrn,nhc->rhc/dot_general | solution.py:82
  973.0 98.5 %fusion.136 = (f32[12,512]{1,0:T(8,128)S(1)}, f32[12,512,4096]{2,1,0:T(8,128)}) fusion(f32[12,512,4096]{2,1,0:T(8,128)} %copy.158, f32[12,512,4096]{2,1,0:T(8,128)} %copy.154, bf16[512,12,64]{0,2,1:T(8,128)(2,1)S(1)} %bitcast.294, bf16[4096,12,64]{0,2,1:T(8,128)(2,1)} %bitcast.280), kind=kOutput, calls=%fused_computation.250 | convolution fusion | flops 3321882624 | bytes 309092352 | tf_op jit(solution)/shard_map/while/body/eval_jaxpr/rhc,nhc->hrn/dot_general | solution.py:58
  1071.4 31.0 %fusion = f32[12,512]{1,0:T(8,128)S(1)} fusion(f32[12,512,4096]{2,1,0:T(8,128)} %get-tuple-element.192, f32[12,512]{1,0:T(8,128)S(1)} %get-tuple-element.191), kind=kLoop, calls=%fused_computation.12 | loop fusion | flops 50325504 | bytes 100712448 | tf_op jit(solution)/shard_map/while/body/eval_jaxpr/reduce_sum | solution.py:80
  1111.1 36.3 %fusion.72 = bf16[12,64,512]{2,1,0:T(8,128)(2,1)} fusion(bf16[4096,12,64]{0,2,1:T(8,128)(2,1)} %bitcast.288, f32[12,512,4096]{2,1,0:T(8,128)} %get-tuple-element.192, f32[12,512]{1,0:T(8,128)S(1)} %fusion, f32[12,512]{1,0:T(8,128)S(1)} %get-tuple-element.191), kind=kOutput, calls=%fused_computation.162 | convolution fusion | flops 3297116160 | bytes 107790336 | tf_op jit(solution)/shard_map/while/body/eval_jaxpr/hrn,nhc->rhc/dot_general | solution.py:82
  1158.8 34.8 %multiply_convert_fusion.3 = (bf16[512,3072]{1,0:T(8,128)(2,1)}, f32[512,3072]{1,0:T(8,128)}, bf16[512,3072]{1,0:T(8,128)(2,1)}, f32[512,3072]{1,0:T(8,128)}, f32[512,3072]{1,0:T(8,128)}) fusion(f32[3072]{0:T(1024)S(1)} %copy-done.100, f32[512,3072]{1,0:T(8,128)S(1)} %fusion.123, bf16[768,3072]{1,0:T(8,128)(2,1)S(1)} %copy-done.113, ...), kind=kOutput, calls=%fused_computation.61 | convolution fusion | flops 2625503232 | bytes 37771264 | tf_op jit(solution)/shard_map/dot_general | solution.py:216
  1227.1 37.7 %fusion.6 = f32[12,64,4096]{2,1,0:T(8,128)} fusion(bf16[512,12,64]{0,2,1:T(8,128)(2,1)S(1)} %bitcast.298, f32[12,512,4096]{2,1,0:T(8,128)} %get-tuple-element.192, f32[12,512]{1,0:T(8,128)S(1)} %log_add_fusion.1), kind=kOutput, calls=%fused_computation.17 | convolution fusion | flops 3271557120 | bytes 114057216 | tf_op jit(solution)/shard_map/while/body/eval_jaxpr/hrn,rhc->nhc/dot_general | solution.py:119
  1264.8 66.3 %multiply_reduce_fusion.1 = (f32[12,512]{1,0:T(8,128)S(1)}, f32[12,512,4096]{2,1,0:T(8,128)}) fusion(f32[12,512,4096]{2,1,0:T(8,128)} %get-tuple-element.192, f32[12,512]{1,0:T(8,128)S(1)} %log_add_fusion.1, bf16[512,12,64]{0,2,1:T(8,128)(2,1)S(1)} %bitcast.299, bf16[4096,12,64]{0,2,1:T(8,128)(2,1)} %bitcast.289), kind=kOutput, calls=%fused_computation.4 | convolution fusion | flops 3296716800 | bytes 208453632 | tf_op jit(solution)/shard_map/while/body/eval_jaxpr/rhc,nhc->hrn/dot_general | solution.py:98
  1331.2 77.8 %multiply_convert_fusion.1 = bf16[12,512,4096]{2,1,0:T(8,128)(2,1)} fusion(f32[12,512,4096]{2,1,0:T(8,128)} %get-tuple-element.200, f32[12,512,4096]{2,1,0:T(8,128)} %get-tuple-element.192, f32[12,512]{1,0:T(8,128)S(1)} %get-tuple-element.199, f32[12,512]{1,0:T(8,128)S(1)} %log_add_fusion.1), kind=kLoop, calls=%fused_computation.3 | loop fusion | flops 100663296 | bytes 251707392 | tf_op jit(solution)/shard_map/while/body/eval_jaxpr/convert_element_type | solution.py:102
  1454.8 75.9 %multiply_reduce_fusion = (f32[12,512]{1,0:T(8,128)S(1)}, f32[12,512,4096]{2,1,0:T(8,128)}) fusion(f32[12,512,4096]{2,1,0:T(8,128)} %get-tuple-element.190, f32[12,512]{1,0:T(8,128)S(1)} %log_add_fusion, bf16[512,12,64]{0,2,1:T(8,128)(2,1)S(1)} %bitcast.296, bf16[4096,12,64]{0,2,1:T(8,128)(2,1)} %bitcast.287), kind=kOutput, calls=%fused_computation.1 | convolution fusion | flops 3296716800 | bytes 208453632 | tf_op jit(solution)/shard_map/while/body/eval_jaxpr/rhc,nhc->hrn/dot_general | solution.py:98
  1530.8 82.6 %multiply_convert_fusion = bf16[12,512,4096]{2,1,0:T(8,128)(2,1)} fusion(f32[12,512,4096]{2,1,0:T(8,128)} %get-tuple-element.202, f32[12,512,4096]{2,1,0:T(8,128)} %get-tuple-element.190, f32[12,512]{1,0:T(8,128)S(1)} %get-tuple-element.201, f32[12,512]{1,0:T(8,128)S(1)} %log_add_fusion), kind=kLoop, calls=%fused_computation | loop fusion | flops 100663296 | bytes 251707392 | tf_op jit(solution)/shard_map/while/body/eval_jaxpr/convert_element_type | solution.py:102
  1637.0 37.7 %fusion.4 = f32[12,64,4096]{2,1,0:T(8,128)} fusion(bf16[512,12,64]{0,2,1:T(8,128)(2,1)S(1)} %bitcast.297, f32[12,512,4096]{2,1,0:T(8,128)} %get-tuple-element.190, f32[12,512]{1,0:T(8,128)S(1)} %log_add_fusion), kind=kOutput, calls=%fused_computation.16 | convolution fusion | flops 3271557120 | bytes 114057216 | tf_op jit(solution)/shard_map/while/body/eval_jaxpr/hrn,rhc->nhc/dot_general | solution.py:119
  1727.4 68.5 %copy.179 = f32[12,512,4096]{1,2,0:T(8,128)} copy(bf16[12,512,4096]{2,1,0:T(8,128)(2,1)} %multiply_convert_fusion) | data formatting | bytes 150994944 | tf_op jit(solution)/shard_map/while/body/eval_jaxpr/convert_element_type | solution.py:108
  1795.9 67.7 %copy.171 = f32[12,512,4096]{1,2,0:T(8,128)} copy(bf16[12,512,4096]{2,1,0:T(8,128)(2,1)} %multiply_convert_fusion.1) | data formatting | bytes 150994944 | tf_op jit(solution)/shard_map/while/body/eval_jaxpr/convert_element_type | solution.py:108
  1920.3 30.9 %bitcast_reduce_fusion = f32[12,512,64]{1,2,0:T(8,128)S(1)} fusion(f32[12,512,4096]{1,2,0:T(8,128)} %copy.179), kind=kLoop, calls=%fused_computation.235 | loop fusion | flops 24772608 | bytes 102236160 | tf_op jit(solution)/shard_map/while/body/eval_jaxpr/reduce_sum | solution.py:108
  2342.2 74.1 %all-reduce.14.cloned.1.call-done = (f32[1536]{0:T(1024)}, f32[768]{0:T(1024)}, f32[3072]{0:T(1024)}, f32[768]{0:T(1024)}, f32[2,768]{1,0:T(2,128)}, /*index=5*/f32[2,768]{1,0:T(2,128)}, f32[2,127,64]{1,2,0:T(8,128)}) async-done(((f32[1536]{0:T(1024)}, f32[768]{0:T(1024)}, f32[3072]{0:T(1024)}, f32[768]{0:T(1024)}, f32[2,768]{1,0:T(2,128)}, /*index=5*/f32[2,768]{1,0:T(2,128)}, f32[2,127,64]{1,2,0:T(8,128)}), ...) | async-done | bytes 101904
  2424.0 98.9 %reduce-scatter.15.cloned.1.call-done = f32[24,768]{1,0:T(8,128)} async-done(((f32[768,768]{1,0:T(8,128)}), f32[24,768]{1,0:T(8,128)}) %reduce-scatter.15.cloned.1.call-update) | async-done | bytes 73744 | tf_op jit(solution)/shard_map/reduce_scatter | solution.py:321
  2522.9 141.2 %reduce-scatter.17.cloned.1.call-done = f32[24,3072]{1,0:T(8,128)} async-done(((f32[768,3072]{1,0:T(8,128)}), f32[24,3072]{1,0:T(8,128)}) %reduce-scatter.17.cloned.1.call-update) | async-done | bytes 294928 | tf_op jit(solution)/shard_map/reduce_scatter | solution.py:323
  2664.2 141.9 %reduce-scatter.19.cloned.1.call-done = f32[96,768]{1,0:T(8,128)} async-done(((f32[3072,768]{1,0:T(8,128)}), f32[96,768]{1,0:T(8,128)}) %reduce-scatter.19.cloned.1.call-update) | async-done | bytes 294928 | tf_op jit(solution)/shard_map/reduce_scatter | solution.py:325
  2806.1 124.3 %reduce-scatter.13.cloned.1.call-done = f32[24,2304]{1,0:T(8,128)} async-done(((f32[768,2304]{1,0:T(8,128)}), f32[24,2304]{1,0:T(8,128)}) %reduce-scatter.13.cloned.1.call-update) | async-done | bytes 221200 | tf_op jit(solution)/shard_map/reduce_scatter | solution.py:319
  (433 shorter events, 793.2 us)
Async XLA Ops:
  7.2 126.3 %all-gather.11.cloned.1.call-start = ((), (), s32[]{:S(2)}) async-start(), calls=%async_computation.6 | async-start | bytes 3649536 | tf_op jit(solution)/shard_map/all_gather | solution.py:28
  7.9 768.7 %all-gather.25.cloned.1.call-start = ((), (), s32[]{:S(2)}) async-start(), calls=%async_computation.13 | async-start | bytes 7077888 | tf_op jit(solution)/shard_map/while/body/eval_jaxpr/all_gather | solution.py:202
  140.0 775.1 %all-gather.23.cloned.1.call-start = ((), (), s32[]{:S(2)}) async-start(), calls=%async_computation.12 | async-start | bytes 7077888 | tf_op jit(solution)/shard_map/while/body/eval_jaxpr/all_gather | solution.py:203
  140.7 818.3 %all-gather.17.cloned.1.call-start = ((), (), s32[]{:S(2)}) async-start(), calls=%async_computation.9 | async-start | bytes 1216512 | tf_op jit(solution)/shard_map/all_gather | solution.py:30
  141.3 822.8 %all-gather.15.cloned.1.call-start = ((), (), s32[]{:S(2)}) async-start(), calls=%async_computation.8 | async-start | bytes 7077888 | tf_op jit(solution)/shard_map/while/body/eval_jaxpr/all_gather | solution.py:202
  147.2 955.3 %all-gather.13.cloned.1.call-start = ((), (), s32[]{:S(2)}) async-start(), calls=%async_computation.7 | async-start | bytes 7077888 | tf_op jit(solution)/shard_map/while/body/eval_jaxpr/all_gather | solution.py:203
  147.7 1003.5 %all-gather.19.cloned.1.call-start = ((), (), s32[]{:S(2)}) async-start(), calls=%async_computation.10 | async-start | bytes 4866048 | tf_op jit(solution)/shard_map/all_gather | solution.py:32
  148.5 1045.1 %all-gather.21.cloned.1.call-start = ((), (), s32[]{:S(2)}) async-start(), calls=%async_computation.11 | async-start | bytes 4866048 | tf_op jit(solution)/shard_map/all_gather | solution.py:34
  149.2 2124.8 %reduce-scatter.9.cloned.1.call-start = ((), (), s32[]{:S(2)}) async-start(), calls=%async_computation.14 | async-start | bytes 28311552 | tf_op jit(solution)/shard_map/while/body/eval_jaxpr/reduce_scatter | solution.py:122
  884.0 39.7 %copy-start.58 = (f32[12,512]{1,0:T(8,128)}, f32[12,512]{1,0:T(8,128)S(1)}, u32[]{:S(2)}) copy-start(f32[12,512]{1,0:T(8,128)S(1)} %get-tuple-element.189) | copy-start | bytes 73732
  923.6 35.4 %copy-start.8 = (bf16[2,512,768]{2,1,0:T(8,128)(2,1)S(1)}, bf16[2,512,768]{2,1,0:T(8,128)(2,1)}, u32[]{:S(2)}) copy-start(bf16[2,512,768]{2,1,0:T(8,128)(2,1)} %param.13) | copy-start | bytes 4718596
  923.7 35.4 %copy-start.109 = (f32[768]{0:T(1024)S(1)}, f32[768]{0:T(1024)}, u32[]{:S(2)}) copy-start(f32[768]{0:T(1024)} %convert_element_type.211) | copy-start | bytes 9220
  1111.1 36.4 %copy-start.9 = (bf16[2,512,768]{2,1,0:T(8,128)(2,1)S(1)}, bf16[2,512,768]{2,1,0:T(8,128)(2,1)}, u32[]{:S(2)}) copy-start(bf16[2,512,768]{2,1,0:T(8,128)(2,1)} %param.13) | copy-start | bytes 4718596
  1111.1 36.4 %copy-start.110 = (f32[768]{0:T(1024)S(1)}, f32[768]{0:T(1024)}, u32[]{:S(2)}) copy-start(f32[768]{0:T(1024)} %convert_element_type.211) | copy-start | bytes 9220
  1150.1 71.3 %copy-start.88 = (f32[512]{0:T(512)}, f32[512]{0:T(512)S(1)}, u32[]{:S(2)}) copy-start(f32[512]{0:T(512)S(1)} %broadcast_multiply_fusion.2) | copy-start | bytes 6148
  1151.2 70.1 %copy-start.103 = (f32[512]{0:T(512)}, f32[512]{0:T(512)S(1)}, u32[]{:S(2)}) copy-start(f32[512]{0:T(512)S(1)} %fusion.107) | copy-start | bytes 6148
  1158.8 34.8 %copy-start.26 = (bf16[2,512,768]{2,1,0:T(8,128)(2,1)S(1)}, bf16[2,512,768]{2,1,0:T(8,128)(2,1)}, u32[]{:S(2)}) copy-start(bf16[2,512,768]{2,1,0:T(8,128)(2,1)} %param.25) | copy-start | bytes 4718596
  1226.0 38.8 %copy-start.49 = (bf16[512,768]{1,0:T(8,128)(2,1)}, bf16[512,768]{1,0:T(8,128)(2,1)S(1)}, u32[]{:S(2)}) copy-start(bf16[512,768]{1,0:T(8,128)(2,1)S(1)} %get-tuple-element.175) | copy-start | bytes 2359300
  1331.2 77.8 %copy-start.23 = (bf16[512,768]{0,1:T(8,128)(2,1)S(1)}, bf16[512,768]{0,1:T(8,128)(2,1)}, u32[]{:S(2)}) copy-start(bf16[512,768]{0,1:T(8,128)(2,1)} %copy-done.21) | copy-start | bytes 2359300
  1451.3 826.1 %reduce-scatter.11.cloned.1.call-start = ((), (), s32[]{:S(2)}) async-start(), calls=%async_computation.15 | async-start | bytes 28311552 | tf_op jit(solution)/shard_map/while/body/eval_jaxpr/reduce_scatter | solution.py:122
  1530.8 82.6 %copy-start.20 = (bf16[512,768]{0,1:T(8,128)(2,1)S(1)}, bf16[512,768]{0,1:T(8,128)(2,1)}, u32[]{:S(2)}) copy-start(bf16[512,768]{0,1:T(8,128)(2,1)} %copy-done.18) | copy-start | bytes 2359300
  1693.4 722.9 %all-reduce.14.cloned.1.call-start = ((), (), s32[]{:S(2)}) async-start(), calls=%async_computation.20 | async-start | bytes 212992
  2127.4 18.4 copy-start.53
  2145.8 28.2 copy-start.1
  2174.1 18.6 copy-start.55
  2192.7 28.8 copy-start.41
  2221.6 25.3 copy-start.40
  2246.9 23.8 copy-start.50
  2289.0 233.9 %reduce-scatter.15.cloned.1.call-start = ((), (), s32[]{:S(2)}) async-start(), calls=%async_computation.17 | async-start | bytes 2433024 | tf_op jit(solution)/shard_map/reduce_scatter | solution.py:321
  2293.0 371.1 %reduce-scatter.17.cloned.1.call-start = ((), (), s32[]{:S(2)}) async-start(), calls=%async_computation.18 | async-start | bytes 9732096 | tf_op jit(solution)/shard_map/reduce_scatter | solution.py:323
  2304.5 501.6 %reduce-scatter.19.cloned.1.call-start = ((), (), s32[]{:S(2)}) async-start(), calls=%async_computation.19 | async-start | bytes 9732096 | tf_op jit(solution)/shard_map/reduce_scatter | solution.py:325
  2314.9 615.4 %reduce-scatter.13.cloned.1.call-start = ((), (), s32[]{:S(2)}) async-start(), calls=%async_computation.16 | async-start | bytes 7299072 | tf_op jit(solution)/shard_map/reduce_scatter | solution.py:319
  (102 other events, 540.9 us)
Sparse Core Ops, SparseCore 0:
  10.9 62.7 all-gather.10
  140.1 47.3 all-gather.24
  189.4 45.5 all-gather.22
  237.7 54.0 all-gather.16
  293.5 44.4 all-gather.14
  339.8 45.5 all-gather.12
  388.2 63.6 all-gather.18
  454.8 62.4 all-gather.20
  1451.4 159.1 reduce-scatter.8
  1693.5 159.1 reduce-scatter.10
  2289.1 127.1 all-reduce.13
  2422.9 100.0 reduce-scatter.14
  2529.4 134.7 reduce-scatter.16
  2671.5 134.5 reduce-scatter.18
  2812.2 118.1 reduce-scatter.12
where the time goes:
time: 2960 us; the launch traced here: 2940 us
  matrix products  979 us (33%)
  local copies, waits for them, and re-layouts  832 us (28%)
  waiting for transfers between devices  585 us (20%)
  other arithmetic  409 us (14%)
  blocking collectives  117 us (4%)
    add x8, local copies, waits for them, and re-layouts, score_block(): product.reshape(HEADS, rows_img, GRID, GRID) + bias_rows[:, :, :, None]  521 us
    dot_general x2, matrix products, score_block(): jnp.einsum('rhc,nhc->hrn', queries, keys_all, preferred_element_type=jnp....  197 us
    convert_element_type x2, other arithmetic, attend_backward(): grad_scores = (probs * (grad_probs - inner_sum)).astype(jnp.bfloat16)  160 us
    dot_general x2, matrix products, attend_backward(): jnp.einsum('rhc,nhc->hrn', grad_heads, values_all, preferred_element_type...  142 us
    reduce_scatter x1, waiting for transfers between devices, body(): lax.psum_scatter(gradients[6], ('dp', 'seq'), scatter_dimension=0, tiled=...  142 us
    reduce_scatter x1, waiting for transfers between devices, body(): lax.psum_scatter(gradients[4], ('dp', 'seq'), scatter_dimension=0, tiled=...  141 us
    convert_element_type x2, local copies, waits for them, and re-layouts, attend_backward(): grad_rows = jnp.sum(grid_scores, axis=3, dtype=jnp.float32)  136 us
    reduce_scatter x1, waiting for transfers between devices, body(): lax.psum_scatter(gradients[0], ('dp', 'seq'), scatter_dimension=0, tiled=...  124 us
  transfers between devices with their start and end apart: 15, of which 5 were waited for; matrix products, arithmetic and copies ran while one was open for 66% of the time, Pallas kernels for 0%

commit v1 on v0

--- a/solution.py
+++ b/solution.py
@@ -1,8 +1,11 @@
 from functools import partial
+import math
 
 import jax
 import jax.numpy as jnp
 from jax import lax
+from jax.experimental import pallas as pl
+from jax.experimental.pallas import tpu as pltpu
 from jax.sharding import PartitionSpec as P
 
 HEADS = 12
@@ -14,6 +17,518 @@
 
 EPS = 1e-06
 HIGH = lax.Precision.HIGHEST
+IMAGES = 8
+AXES = ("dp", "seq")
+
+TB = 512
+CK = 512
+ROWS = CK // GRID
+LOG2E = 1.4426950408889634
+NN = (((1,), (0,)), ((), ()))
+NT = (((1,), (1,)), ((), ()))
+TN = (((0,), (0,)), ((), ()))
+BF = jnp.bfloat16
+F32 = jnp.float32
+
+
+def dot(a, b, dims):
+    return lax.dot_general(a, b, dims, preferred_element_type=F32)
+
+
+def col_hot(n):
+    key = lax.broadcasted_iota(jnp.int32, (n, GRID), 0) & (GRID - 1)
+    col = lax.broadcasted_iota(jnp.int32, (n, GRID), 1)
+    return (key == col).astype(F32)
+
+
+def build_keys(qkv_ref, kaug, start, n):
+    rows = pl.ds(start, n)
+    k = qkv_ref[rows, HD : 2 * HD].astype(F32)
+    pair = jnp.concatenate([k, col_hot(n)], axis=1).astype(BF)
+    kaug[rows, : 2 * HD] = pair
+    kaug[rows, 2 * HD :] = pair
+
+
+def fwd_kernel(n_chunks, qkv_ref, tab_ref, oT_ref, oTf_ref, qaT_ref, sub_ref, kaug, vta):
+    i = pl.program_id(0)
+    tg = TB // GRID
+
+    @pl.when(i == 0)
+    def _():
+        for c in range(n_chunks):
+            build_keys(qkv_ref, kaug, c * CK, CK)
+            rows = pl.ds(c * CK, CK)
+            vT = qkv_ref[rows, 2 * HD :].astype(F32).T
+            vta[0:HD, rows] = vT.astype(BF)
+            one = lax.broadcasted_iota(jnp.int32, (16, CK), 0) == 0
+            vta[HD : HD + 16, rows] = one.astype(F32).astype(BF)
+
+    q = qkv_ref[pl.ds(pl.multiple_of(i * TB, TB), TB), :HD]
+    gr = dot(q, tab_ref[0], NT) * LOG2E
+    gc = dot(q, tab_ref[1], NT) * LOG2E
+    brs, bcs = [], []
+    for g in range(tg):
+        sl = slice(g * GRID, (g + 1) * GRID)
+        brs.append(pltpu.roll(gr[sl], i * tg + g, 1))
+        bcs.append(pltpu.roll(gc[sl], 0, 1, stride=1, stride_axis=0))
+    br = jnp.concatenate(brs, axis=0)
+    bc = jnp.concatenate(bcs, axis=0)
+    qs = q.astype(F32) * (HD ** -0.5 * LOG2E)
+    cat = jnp.concatenate([qs, bc[:, :GRID]], axis=1).T
+    hi = cat.astype(BF)
+    lo = (cat - hi.astype(F32)).astype(BF)
+    qaT_ref[...] = jnp.concatenate([hi, lo], axis=0)
+    sub_ref[...] = br.T[:GRID]
+    qa = qaT_ref[...]
+
+    m = jnp.full((1, TB), -jnp.inf, F32)
+    acc = jnp.zeros((HD + 16, TB), F32)
+    for c in range(n_chunks):
+        s = dot(kaug[c * CK : (c + 1) * CK, :], qa, NN).reshape(ROWS, GRID, TB)
+        b8 = sub_ref[c * ROWS : (c + 1) * ROWS, :]
+        mc = jnp.max(jnp.max(s, axis=1) + b8, axis=0, keepdims=True)
+        p = jnp.exp2(s - (mc - b8)[:, None, :]).astype(BF).reshape(CK, TB)
+        o = dot(vta[:, c * CK : (c + 1) * CK], p, NN)
+        new = jnp.maximum(m, mc)
+        acc = acc * jnp.exp2(m - new) + o * jnp.exp2(mc - new)
+        m = new
+    total = acc[HD : HD + 1]
+    out = acc[:HD] / total
+    oT_ref[0] = out.astype(BF)
+    oTf_ref[...] = out
+    sub_ref[...] = (m + jnp.log2(total)) - sub_ref[...]
+
+
+def heads_forward(qkv, tab):
+    n = qkv.shape[0]
+    steps = n // TB
+    return pl.pallas_call(
+        partial(fwd_kernel, n // CK),
+        grid=(steps,),
+        in_specs=[
+            pl.BlockSpec((n, 3 * HD), lambda i: (0, 0)),
+            pl.BlockSpec((2, 2 * GRID, HD), lambda i: (0, 0, 0)),
+        ],
+        out_specs=[
+            pl.BlockSpec((1, HD, TB), lambda i: (i, 0, 0)),
+            pl.BlockSpec((HD, TB), lambda i: (0, i)),
+            pl.BlockSpec((4 * HD, TB), lambda i: (0, i)),
+            pl.BlockSpec((GRID, TB), lambda i: (0, i)),
+        ],
+        out_shape=[
+            jax.ShapeDtypeStruct((steps, HD, TB), BF),
+            jax.ShapeDtypeStruct((HD, n), F32),
+            jax.ShapeDtypeStruct((4 * HD, n), BF),
+            jax.ShapeDtypeStruct((GRID, n), F32),
+        ],
+        scratch_shapes=[pltpu.VMEM((n, 4 * HD), BF), pltpu.VMEM((HD + 16, n), BF)],
+        compiler_params=pltpu.CompilerParams(vmem_limit_bytes=56 * 2**20),
+        cost_estimate=pl.CostEstimate(
+            flops=4 * n * n * 4 * HD, bytes_accessed=16 * 2**20, transcendentals=n * n
+        ),
+    )(qkv, tab)
+
+
+def bwd_kernel(
+    n_chunks, qkv_ref, tab_ref, qaT_ref, sub_ref, oTf_ref, doT_ref,
+    dqkv_ref, dtab_ref, kaug, vaug, kta, dkv, dqa
+):
+    i = pl.program_id(0)
+    tg = TB // GRID
+    n_steps = pl.num_programs(0)
+
+    @pl.when(i == 0)
+    def _():
+        for c in range(n_chunks):
+            build_keys(qkv_ref, kaug, c * CK, CK)
+            rows = pl.ds(c * CK, CK)
+            k = qkv_ref[rows, HD : 2 * HD].astype(F32)
+            both = jnp.concatenate([k, col_hot(CK)], axis=1).T
+            kta[0 : 2 * HD, rows] = both.astype(BF)
+            key = lax.broadcasted_iota(jnp.int32, (16, CK), 1) >> 6
+            hot = lax.broadcasted_iota(jnp.int32, (16, CK), 0) == key
+            kta[2 * HD : 2 * HD + 16, rows] = hot.astype(F32).astype(BF)
+            v = qkv_ref[rows, 2 * HD :].astype(F32)
+            lane = lax.broadcasted_iota(jnp.int32, (CK, HD), 1)
+            vaug[rows, :] = jnp.concatenate([v, (lane < 3).astype(F32)], axis=1).astype(BF)
+            dkv[rows, :] = jnp.zeros((CK, 2 * HD), F32)
+        dtab_ref[...] = jnp.zeros_like(dtab_ref)
+
+    q = qkv_ref[pl.ds(pl.multiple_of(i * TB, TB), TB), :HD]
+    doT = doT_ref[0].astype(F32)
+    delta = -jnp.sum(doT * oTf_ref[...], axis=0, keepdims=True)
+    d1 = delta.astype(BF)
+    r1 = delta - d1.astype(F32)
+    d2 = r1.astype(BF)
+    d3 = (r1 - d2.astype(F32)).astype(BF)
+    pad = jnp.concatenate(
+        [d1.astype(F32), d2.astype(F32), d3.astype(F32), jnp.zeros((HD - 3, TB), F32)], axis=0
+    )
+    doa = jnp.concatenate([doT, pad], axis=0).astype(BF)
+    do = jnp.concatenate([doT, jnp.zeros((HD, TB), F32)], axis=0).T
+    qz = jnp.concatenate([jnp.zeros((TB, HD), F32), q.astype(F32)], axis=1)
+    doq = jnp.concatenate([do, qz], axis=0).astype(BF)
+    qa = qaT_ref[...]
+    dqa[...] = jnp.zeros_like(dqa)
+
+    for c in range(n_chunks):
+        rows = slice(c * CK, (c + 1) * CK)
+        s = dot(kaug[rows, :], qa, NN).reshape(ROWS, GRID, TB)
+        b8 = sub_ref[c * ROWS : (c + 1) * ROWS, :]
+        p = jnp.exp2(s - b8[:, None, :]).reshape(CK, TB)
+        dp = dot(vaug[rows, :], doa, NN)
+        ds = (p * dp).astype(BF)
+        pd = jnp.concatenate([p.astype(BF), ds], axis=1)
+        dkv[rows, :] += dot(pd, doq, NN)
+        g = dot(kta[:, rows], ds, NN)
+        dqa[0 : 2 * HD, :] += g[: 2 * HD]
+        dqa[2 * HD + c * ROWS : 2 * HD + (c + 1) * ROWS, :] = g[2 * HD : 2 * HD + ROWS]
+
+    grads = dqa[HD : 3 * HD, :].T
+    lane = lax.broadcasted_iota(jnp.int32, (TB, 2 * GRID), 1)
+    gcol = jnp.where(lane < GRID, grads, 0.0)
+    grow = jnp.where(lane >= GRID, grads, 0.0)
+    rs, cs = [], []
+    col = lax.broadcasted_iota(jnp.int32, (GRID, 2 * GRID), 0)
+    for g in range(tg):
+        sl = slice(g * GRID, (g + 1) * GRID)
+        rs.append(pltpu.roll(grow[sl], GRID - (i * tg + g), 1))
+        x = gcol[sl]
+        for bit in range(6):
+            x = jnp.where((col >> bit) & 1 == 1, pltpu.roll(x, 2 * GRID - (1 << bit), 1), x)
+        cs.append(x)
+    drow = jnp.concatenate(rs, axis=0).astype(BF)
+    dcol = jnp.concatenate(cs, axis=0).astype(BF)
+    dq = dqa[:HD, :] * HD ** -0.5
+    dq = dq + dot(tab_ref[0], drow, (((0,), (1,)), ((), ())))
+    dq = dq + dot(tab_ref[1], dcol, (((0,), (1,)), ((), ())))
+    dqkv_ref[i, 0:HD, :] = dq.astype(BF)
+    dtab_ref[0] += dot(q, drow, TN)
+    dtab_ref[1] += dot(q, dcol, TN)
+
+    @pl.when(i == n_steps - 1)
+    def _():
+        for c in range(n_chunks):
+            both = dkv[c * CK : (c + 1) * CK, :].T
+            dqkv_ref[c, HD : 2 * HD, :] = (both[HD:] * HD ** -0.5).astype(BF)
+            dqkv_ref[c, 2 * HD :, :] = both[:HD].astype(BF)
+
+
+def heads_backward(qkv, tab, qaT, sub, oTf, doT):
+    n = qkv.shape[0]
+    steps = n // TB
+    return pl.pallas_call(
+        partial(bwd_kernel, n // CK),
+        grid=(steps,),
+        in_specs=[
+            pl.BlockSpec((n, 3 * HD), lambda i: (0, 0)),
+            pl.BlockSpec((2, 2 * GRID, HD), lambda i: (0, 0, 0)),
+            pl.BlockSpec((4 * HD, TB), lambda i: (0, i)),
+            pl.BlockSpec((GRID, TB), lambda i: (0, i)),
+            pl.BlockSpec((HD, TB), lambda i: (0, i)),
+            pl.BlockSpec((1, HD, TB), lambda i: (i, 0, 0)),
+        ],
+        out_specs=[
+            pl.BlockSpec((steps, 3 * HD, TB), lambda i: (0, 0, 0)),
+            pl.BlockSpec((2, HD, 2 * GRID), lambda i: (0, 0, 0)),
+        ],
+        out_shape=[
+            jax.ShapeDtypeStruct((steps, 3 * HD, TB), BF),
+            jax.ShapeDtypeStruct((2, HD, 2 * GRID), F32),
+        ],
+        scratch_shapes=[
+            pltpu.VMEM((n, 4 * HD), BF),
+            pltpu.VMEM((n, 2 * HD), BF),
+            pltpu.VMEM((2 * HD + 16, n), BF),
+            pltpu.VMEM((n, 2 * HD), F32),
+            pltpu.VMEM((3 * HD, TB), F32),
+        ],
+        compiler_params=pltpu.CompilerParams(vmem_limit_bytes=56 * 2**20),
+        cost_estimate=pl.CostEstimate(
+            flops=10 * n * n * 4 * HD, bytes_accessed=20 * 2**20, transcendentals=n * n
+        ),
+    )(qkv, tab, qaT, sub, oTf, doT)
+
+
+def mirror(tables):
+    hole = jnp.zeros((2, 1, HD), tables.dtype)
+    return jnp.concatenate([tables[:, GRID - 1 :: -1], hole, tables[:, : GRID - 1 : -1]], axis=1)
+
+
+def unmirror(grads):
+    return jnp.concatenate([grads[:, GRID - 1 :: -1], grads[:, : GRID : -1]], axis=1)
+
+
+def swap(block, bit, size):
+    return lax.ppermute(block, "seq", [(i, i ^ bit) for i in range(size)])
+
+
+def spread(vector, size):
+    return lax.all_to_all(
+        jnp.broadcast_to(vector[None], (size,) + vector.shape), AXES, 0, 0, tiled=True
+    )
+
+
+def reduce_pieces(pieces):
+    size, n = pieces.shape
+    padded = jnp.pad(pieces, ((0, 0), (0, 1024 - n))).reshape(size, 8, 128)
+    got = lax.all_to_all(padded, AXES, 0, 0, tiled=True)
+    return jnp.sum(got, axis=0).reshape(1024)[:n]
+
+
+def norm_parts(values):
+    center = jnp.mean(values, axis=-1, keepdims=True)
+    centered = values - center
+    rate = lax.rsqrt(jnp.mean(centered * centered, axis=-1, keepdims=True) + EPS)
+    return centered * rate, rate
+
+
+def norm_back(grad, hat, rate, gain):
+    u = grad * gain
+    return rate * (
+        u
+        - jnp.mean(u, axis=-1, keepdims=True)
+        - hat * jnp.mean(u * hat, axis=-1, keepdims=True)
+    )
+
+
+def body_heads(
+    tokens,
+    w_qkv,
+    qv_bias,
+    w_proj,
+    proj_bias,
+    w_fc1,
+    fc1_bias,
+    w_fc2,
+    fc2_bias,
+    norm_gains,
+    norm_biases,
+    rel_tables,
+    cotangent,
+):
+    images, rows_img, features = tokens.shape
+    dps, seqs = lax.axis_size("dp"), lax.axis_size("seq")
+    size = dps * seqs
+    slots = seqs // images
+    per = HEADS // slots
+    part = features // size
+    wide = per * 3 * HD
+    hidden = fc1_bias.shape[0] * size
+    blocks = hidden // features
+    here = lax.axis_index("seq")
+    image, slot = here // slots, here % slots
+    rows = images * rows_img
+
+    own = lax.dynamic_index_in_dim(tokens, image, 0, keepdims=False)
+    other = lax.dynamic_index_in_dim(tokens, 1 - image, 0, keepdims=False)
+    got = swap(other, 4, seqs)
+    near = [own, swap(own, 2, seqs), got, swap(got, 2, seqs)]
+    far = [swap(block, 1, seqs) for block in near]
+    by_mask = jnp.stack([near[0], far[0], near[1], far[1], near[2], far[2], near[3], far[3]])
+    image_tokens = jnp.concatenate(
+        [lax.dynamic_index_in_dim(by_mask, j ^ here, 0, keepdims=True) for j in range(seqs)]
+    )
+
+    small = jnp.concatenate(
+        [
+            qv_bias,
+            proj_bias,
+            fc1_bias,
+            fc2_bias,
+            norm_gains.reshape(-1),
+            norm_biases.reshape(-1),
+        ]
+    )
+    lengths = [2 * part, part, blocks * part, part, 2 * part, 2 * part]
+    small = jnp.pad(small, (0, 1024 - small.shape[0])).reshape(8, 128)
+    smalls = spread(small, size).reshape(size, 1024)
+    edges = [sum(lengths[:j]) for j in range(len(lengths) + 1)]
+    cut = [smalls[:, a:b].astype(F32) for a, b in zip(edges[:-1], edges[1:])]
+    bqv, bp, b2 = cut[0].reshape(-1), cut[1].reshape(-1), cut[3].reshape(-1)
+    b1 = cut[2].reshape(size, blocks, part).transpose(1, 0, 2).reshape(-1)
+    gains = cut[4].reshape(size, 2, part).transpose(1, 0, 2).reshape(2, features)
+    shifts = cut[5].reshape(size, 2, part).transpose(1, 0, 2).reshape(2, features)
+
+    by_head = w_qkv.reshape(part, 3, slots, per, HD)
+    to_slots = by_head.transpose(2, 0, 3, 1, 4).reshape(slots, part, wide)
+    cols = lax.all_to_all(
+        jnp.concatenate([to_slots] * images, axis=0), "seq", 0, 0, tiled=True
+    ).reshape(seqs * part, wide)
+    w_cols = lax.all_gather(cols, "dp", axis=0, tiled=True)
+
+    w1_local = w_fc1.reshape(part, size, blocks, part).transpose(0, 2, 1, 3).reshape(part, hidden)
+    w2_local = w_fc2.reshape(blocks, part, features).transpose(1, 0, 2).reshape(part, hidden)
+    wq_local = by_head.transpose(0, 3, 2, 1, 4).reshape(part, 3 * features)
+    whole = lax.all_gather(
+        jnp.concatenate([w1_local, w2_local, w_proj, wq_local], axis=1), AXES, axis=0, tiled=True
+    )
+    w1 = whole[:, :hidden]
+    w2 = (
+        whole[:, hidden : 2 * hidden]
+        .reshape(features, blocks, features)
+        .transpose(1, 0, 2)
+        .reshape(hidden, features)
+    )
+    wp = whole[:, 2 * hidden : 2 * hidden + features]
+    wq = whole[:, 2 * hidden + features :]
+
+    length = seqs * rows_img
+    hat_all, _ = norm_parts(image_tokens.reshape(length, features).astype(F32))
+    normed_all = (hat_all * gains[0] + shifts[0]).astype(BF)
+    full_bias = jnp.stack(
+        [
+            bqv[:features].reshape(slots, per, HD),
+            jnp.zeros((slots, per, HD), F32),
+            bqv[features:].reshape(slots, per, HD),
+        ],
+        axis=2,
+    ).reshape(slots, wide)
+    own_bias = lax.dynamic_index_in_dim(full_bias, slot, 0, keepdims=False)
+    qkv = (dot(normed_all, w_cols, NN) + own_bias).astype(BF)
+
+    tab = mirror(rel_tables)
+    kept, arrived = [], []
+    for p in range(per):
+        qkv_p = qkv[:, p * 3 * HD : (p + 1) * 3 * HD]
+        out, *saved = heads_forward(qkv_p, tab)
+        kept.append([qkv_p, tab, saved[1], saved[2], saved[0]])
+        back = lax.all_to_all(out, "seq", 0, 0, tiled=True)
+        arrived.append(back.reshape(images, slots, 1, HD, rows_img))
+    attendedT = jnp.concatenate(arrived, axis=2).reshape(images, features, rows_img)
+
+    inputs = tokens.astype(F32)
+    mixed = inputs + jnp.einsum("yht,hc->ytc", attendedT, wp, preferred_element_type=F32) + bp
+    mixed = mixed.reshape(rows, features)
+    hat2, rate2 = norm_parts(mixed)
+    normed2 = (hat2 * gains[1] + shifts[1]).astype(BF)
+    pre = dot(normed2, w1, NN) + b1
+    cdf = 0.5 * (1.0 + lax.erf(pre * 0.5**0.5))
+    activated = (pre * cdf).astype(BF)
+    slope = cdf + pre * jnp.exp(-0.5 * pre * pre) * (2.0 * math.pi) ** -0.5
+    result = (mixed + dot(activated, w2, NN) + b2).astype(BF).reshape(tokens.shape)
+
+    grad_out = cotangent.reshape(rows, features)
+    grad_out_f = grad_out.astype(F32)
+    grad_pre = (dot(grad_out, w2, NT) * slope).astype(BF)
+    grad_norm2 = dot(grad_pre, w1, NT)
+    grad_mixed = grad_out_f + norm_back(grad_norm2, hat2, rate2, gains[1])
+    grad_branch = grad_mixed.astype(BF)
+    grad_attT = jnp.einsum(
+        "hc,ytc->yht",
+        wp,
+        grad_branch.reshape(images, rows_img, features),
+        preferred_element_type=F32,
+    ).astype(BF)
+    grad_attT = grad_attT.reshape(images * slots, per, HD, rows_img)
+    grad_w2 = dot(activated, grad_out, TN).astype(BF)
+    grad_w2 = (
+        grad_w2.reshape(blocks, features, features).transpose(1, 0, 2).reshape(features, hidden)
+    )
+    grad_w1 = dot(normed2, grad_pre, TN).astype(BF)
+    grad_wp = jnp.einsum(
+        "yht,ytc->hc",
+        attendedT,
+        grad_branch.reshape(images, rows_img, features),
+        preferred_element_type=F32,
+    ).astype(BF)
+    summed = lax.psum_scatter(
+        jnp.concatenate([grad_w1, grad_w2, grad_wp], axis=1), AXES, scatter_dimension=0, tiled=True
+    ).astype(F32)
+    w_fc1_grad = (
+        summed[:, :hidden].reshape(part, blocks, size, part).transpose(0, 2, 1, 3)
+    ).reshape(part, hidden)
+    w_fc2_grad = (
+        summed[:, hidden : 2 * hidden].reshape(part, blocks, features).transpose(1, 0, 2)
+    ).reshape(blocks * part, features)
+    w_proj_grad = summed[:, 2 * hidden :]
+    grad_b1 = jnp.sum(grad_pre, axis=0, dtype=F32)
+    grad_b1 = grad_b1.reshape(blocks, size, part).transpose(1, 0, 2).reshape(size, blocks * part)
+    bundle = jnp.concatenate(
+        [
+            jnp.sum(grad_branch, axis=0, dtype=F32).reshape(size, part),
+            grad_b1,
+            jnp.sum(grad_out_f, axis=0).reshape(size, part),
+            jnp.sum(grad_norm2 * hat2, axis=0).reshape(size, part),
+            jnp.sum(grad_norm2, axis=0).reshape(size, part),
+        ],
+        axis=1,
+    )
+    bundle = reduce_pieces(bundle)
+    proj_bias_grad = bundle[:part]
+    fc1_bias_grad = bundle[part : (1 + blocks) * part]
+    fc2_bias_grad = bundle[(1 + blocks) * part : (2 + blocks) * part]
+    gain1_grad = bundle[(2 + blocks) * part : (3 + blocks) * part]
+    shift1_grad = bundle[(3 + blocks) * part : (4 + blocks) * part]
+
+    grad_norm1 = jnp.zeros((images, rows_img, features), F32)
+    table_sum = jnp.zeros((2, HD, 2 * GRID), F32)
+    weight_grads, bias_sums = [], []
+    for p in range(per):
+        do_p = lax.all_to_all(grad_attT[:, p], "seq", 0, 0, tiled=True)
+        dqkv, dtab = heads_backward(*kept[p], do_p)
+        table_sum = table_sum + dtab
+        sent = lax.all_to_all(dqkv, "seq", 0, 0, tiled=True)
+        sent = sent.reshape(images, slots * 3 * HD, rows_img)
+        own_cols = wq[:, p * slots * 3 * HD : (p + 1) * slots * 3 * HD]
+        grad_norm1 = grad_norm1 + jnp.einsum(
+            "yht,ch->ytc", sent, own_cols, preferred_element_type=F32
+        )
+        bias_sums.append(
+            jnp.sum(sent, axis=(0, 2), dtype=F32).reshape(slots, 3, HD)
+        )
+        grad_w = jnp.einsum(
+            "sct,sjt->cj",
+            normed_all.reshape(seqs, rows_img, features).swapaxes(1, 2),
+            dqkv,
+            preferred_element_type=F32,
+        )
+        grad_w = grad_w.reshape(dps, seqs, part, 3 * HD).swapaxes(0, 1)
+        grad_w = lax.all_to_all(grad_w, "seq", 0, 0, tiled=True)
+        grad_w = jnp.sum(grad_w.reshape(images, slots, dps, part, 3 * HD), axis=0).swapaxes(0, 1)
+        grad_w = lax.all_to_all(grad_w, "dp", 0, 0, tiled=True)
+        weight_grads.append(jnp.sum(grad_w, axis=0).reshape(slots, part, 3, HD))
+    w_qkv_grad = jnp.stack(weight_grads, axis=1).transpose(2, 3, 0, 1, 4).reshape(part, 3 * features)
+
+    hat1, rate1 = norm_parts(inputs)
+    tokens_grad = grad_mixed.reshape(tokens.shape) + norm_back(grad_norm1, hat1, rate1, gains[0])
+    tokens_grad = tokens_grad.astype(BF)
+    bias_sum = jnp.stack(bias_sums, axis=1)
+    bundle = jnp.concatenate(
+        [
+            jnp.concatenate([bias_sum[:, :, 0].reshape(-1), bias_sum[:, :, 2].reshape(-1)]).reshape(
+                size, 2 * part
+            ),
+            jnp.sum(grad_norm1 * hat1, axis=(0, 1)).reshape(size, part),
+            jnp.sum(grad_norm1, axis=(0, 1)).reshape(size, part),
+        ],
+        axis=1,
+    )
+    bundle = reduce_pieces(bundle)
+    qv_bias_grad = bundle[: 2 * part]
+    norm_gains_grad = jnp.stack([bundle[2 * part : 3 * part], gain1_grad])
+    norm_biases_grad = jnp.stack([bundle[3 * part : 4 * part], shift1_grad])
+
+    chunk = 2 * HD * 2 * GRID // size
+    mine = reduce_pieces(table_sum.reshape(size, chunk))
+    shared = spread(jnp.pad(mine, (0, 1024 - chunk)).reshape(8, 128), size)
+    table_all = shared.reshape(size, 1024)[:, :chunk].reshape(2, HD, 2 * GRID)
+    rel_tables_grad = unmirror(table_all.swapaxes(1, 2))
+    return (
+        result,
+        tokens_grad,
+        w_qkv_grad,
+        qv_bias_grad,
+        w_proj_grad,
+        proj_bias_grad,
+        w_fc1_grad,
+        fc1_bias_grad,
+        w_fc2_grad,
+        fc2_bias_grad,
+        norm_gains_grad,
+        norm_biases_grad,
+        rel_tables_grad,
+    )
 
 
 def layer_norm(values, gain, shift):
@@ -367,8 +882,10 @@
         P(),
         P("dp", "seq", None),
     )
+    seqs, images = mesh.shape["seq"], IMAGES // mesh.shape["dp"]
+    by_heads = seqs == 8 and images == 2
     return jax.shard_map(
-        body,
+        body_heads if by_heads else body,
         mesh=mesh,
         in_specs=placed,
         out_specs=(

time: 2960 us -> 771 us (0.26)
  matrix products: 979 us -> 99.6 us
  local copies, waits for them, and re-layouts: 832 us -> 78 us
  waiting for transfers between devices: 585 us -> 97.1 us
  other arithmetic: 409 us -> 44.2 us
  Pallas kernels: 0 us -> 278 us
  starting transfers between devices: 1.06 us -> 81.7 us
  blocking collectives: 117 us -> 67.4 us
    dot_general x52 -> x16, matrix products: 979 us -> 99.6 us  [the longest x7 60.5 us: dot(): return lax.dot_general(a, b, dims, preferred_element_type=F32)]
    add x8 -> x7, local copies, waits for them, and re-layouts: 521 us -> 1.12 us  [the longest x1 0.68 us: body_heads(): mixed + dot(activated, w2, NN) + b2]
    reduce_scatter x6 -> x1, waiting for transfers between devices: 506 us -> 0.01 us  [body_heads(): lax.psum_scatter(jnp.concatenate([grad_w1, grad_w2, grad_wp], axis=1), AX...]
    pallas_call x0 -> x6, Pallas kernels: none -> 278 us  [the longest x3 159 us: heads_backward(): pl.pallas_call(partial(bwd_kernel, n // CK), grid=(steps,), in_specs=[pl....]
    reduce_sum x17 -> x22, other arithmetic: 196 us -> 19 us  [the longest x3 4.33 us: norm_parts(): jnp.mean(centered * centered, axis=-1, keepdims=True) + EPS]
    convert_element_type x10 -> x1, local copies, waits for them, and re-layouts: 163 us -> 1.71 us  [body_heads(): grad_attT = jnp.einsum('hc,ytc->yht', wp, grad_branch.reshape(images, row...]
    convert_element_type x6 -> x4, other arithmetic: 162 us -> 7.8 us  [the longest x1 4.29 us: body_heads(): tokens_grad = tokens_grad.astype(BF)]
    all_to_all x0 -> x19, waiting for transfers between devices: none -> 97.1 us  [the longest x3 22 us: body_heads(): grad_w = lax.all_to_all(grad_w, 'seq', 0, 0, tiled=True)]
  transfers between devices with their start and end apart: 15 -> 28, of which waited for: 5 -> 14; matrix products, arithmetic and copies ran while one was open for 66% -> 19% of each run, Pallas kernels for 0% -> 36%
where the time goes in v1:
time: 771 us; the launch traced here: 761 us
  Pallas kernels  278 us (36%)
  matrix products  99.6 us (13%)
  waiting for transfers between devices  97.1 us (13%)
  starting transfers between devices  81.7 us (11%)
  local copies, waits for them, and re-layouts  78 us (10%)
  blocking collectives  67.4 us (9%)
  other arithmetic  44.2 us (6%)
  between operations  15.7 us (2%)
    pallas_call x3, Pallas kernels, heads_backward(): pl.pallas_call(partial(bwd_kernel, n // CK), grid=(steps,), in_specs=[pl....  159 us
    pallas_call x3, Pallas kernels, heads_forward(): pl.pallas_call(partial(fwd_kernel, n // CK), grid=(steps,), in_specs=[pl....  118 us
    dot_general x7, matrix products, dot(): return lax.dot_general(a, b, dims, preferred_element_type=F32)  60.5 us
    all_to_all x1, blocking collectives, body_heads(): sent = lax.all_to_all(dqkv, 'seq', 0, 0, tiled=True)  29.4 us
    unnamed x127, local copies, waits for them, and re-layouts  29 us
    all_gather x1, blocking collectives, body_heads(): w_cols = lax.all_gather(cols, 'dp', axis=0, tiled=True)  26.1 us
    all_to_all x3, waiting for transfers between devices, body_heads(): grad_w = lax.all_to_all(grad_w, 'seq', 0, 0, tiled=True)  22 us
    dot_general x3, matrix products, body_heads(): jnp.einsum('sct,sjt->cj', normed_all.reshape(seqs, rows_img, features).sw...  18.7 us
  transfers between devices with their start and end apart: 28, of which 14 were waited for; matrix products, arithmetic and copies ran while one was open for 19% of the time, Pallas kernels for 36%

profile of v1, /device:TPU:0, one launch (start us, length us, event | category | flops | bytes accessed | tf_op | source)
XLA Modules:
  0.0 761.4 jit_solution(14582263148199839605)
XLA Ops:
  33.0 10.1 %all-to-all-done = bf16[32,8,128]{2,1,0:T(8,128)(2,1)S(1)} async-done(((bf16[32,8,128]{2,1,0:T(8,128)(2,1)}), bf16[32,8,128]{2,1,0:T(8,128)(2,1)S(1)}, u32[]{:S(2)}, u32[]{:S(2)}) %all-to-all-start) | async-done | bytes 65568 | tf_op jit(solution)/shard_map/all_to_all | solution.py:267
  49.8 5.5 all-to-all-done.1
  55.3 26.1 %all_gather.6 = bf16[768,576]{1,0:T(8,128)(2,1)S(1)} all-gather(bf16[192,576]{1,0:T(8,128)(2,1)S(1)} %bitcast.276), channel_id=1, replica_groups=mesh['dp'=4,'seq'=8] {'dp'}, dimensions={0}, use_global_device_ids=true | all-gather | bytes 1105920 | tf_op jit(solution)/shard_map/all_gather | solution.py:358
  105.0 5.3 add_convert_fusion.1
  114.1 39.5 %shard_map.228 = (bf16[8,64,512]{2,1,0:T(8,128)(2,1)}, f32[64,4096]{1,0:T(8,128)}, bf16[256,4096]{1,0:T(8,128)(2,1)}, f32[64,4096]{1,0:T(8,128)}) custom-call(bf16[4096,192]{1,0:T(8,128)(2,1)} %get-tuple-element.60.qkv_ref, bf16[2,128,64]{2,1,0:T(8,128)(2,1)} %pad_maximum_fusion.4.tab_ref), custom_call_target="tpu_custom_call" | custom-call | flops 17179869184 | bytes 16777216 | tf_op jit(solution)/shard_map/pallas_call | solution.py:105
  153.6 5.0 all-to-all-start.2
  158.6 39.5 %shard_map.229 = (bf16[8,64,512]{2,1,0:T(8,128)(2,1)}, f32[64,4096]{1,0:T(8,128)}, bf16[256,4096]{1,0:T(8,128)(2,1)}, f32[64,4096]{1,0:T(8,128)}) custom-call(bf16[4096,192]{1,0:T(8,128)(2,1)} %get-tuple-element.62.qkv_ref, bf16[2,128,64]{2,1,0:T(8,128)(2,1)} %pad_maximum_fusion.4.tab_ref), custom_call_target="tpu_custom_call" | custom-call | flops 17179869184 | bytes 16777216 | tf_op jit(solution)/shard_map/pallas_call | solution.py:105
  202.2 39.5 %shard_map.230 = (bf16[8,64,512]{2,1,0:T(8,128)(2,1)}, f32[64,4096]{1,0:T(8,128)}, bf16[256,4096]{1,0:T(8,128)(2,1)}, f32[64,4096]{1,0:T(8,128)}) custom-call(bf16[4096,192]{1,0:T(8,128)(2,1)} %get-tuple-element.61.qkv_ref, bf16[2,128,64]{2,1,0:T(8,128)(2,1)} %pad_maximum_fusion.4.tab_ref), custom_call_target="tpu_custom_call" | custom-call | flops 17179869184 | bytes 16777216 | tf_op jit(solution)/shard_map/pallas_call | solution.py:105
  247.5 8.3 %all-to-all-done.4 = bf16[8,64,512]{2,1,0:T(8,128)(2,1)S(1)} async-done(((bf16[8,64,512]{2,1,0:T(8,128)(2,1)}), bf16[8,64,512]{2,1,0:T(8,128)(2,1)S(1)}, u32[]{:S(2)}, u32[]{:S(2)}) %all-to-all-start.4) | async-done | bytes 524320 | tf_op jit(solution)/shard_map/all_to_all | solution.py:396
  267.2 9.8 %multiply_convert_fusion = (bf16[1024,3072]{1,0:T(8,128)(2,1)}, f32[1024,3072]{1,0:T(8,128)}) fusion(f32[3072]{0:T(1024)S(1)} %reshape.418, bf16[1024,768]{1,0:T(8,128)(2,1)S(1)} %add_convert_fusion.2, bf16[768,9216]{1,0:T(8,128)(2,1)S(1)} %bitcast.245), kind=kOutput, calls=%fused_computation.14 | convolution fusion | flops 4850712576 | bytes 25178112 | tf_op jit(solution)/shard_map/dot_general | solution.py:35
  277.0 12.2 %convert_reduce_fusion = (f32[3072]{0:T(1024)}, bf16[1024,3072]{1,0:T(8,128)(2,1)S(1)}) fusion(f32[1024,3072]{1,0:T(8,128)} %get-tuple-element.99, f32[3072]{0:T(1024)S(1)} %reshape.418, bf16[3072,768]{1,0:T(8,128)(2,1)S(1)} %bitcast.257, bf16[1024,768]{1,0:T(8,128)(2,1)S(1)} %bitcast.252), kind=kOutput, calls=%fused_computation.12 | convolution fusion | flops 4872729600 | bytes 25190400 | tf_op jit(solution)/shard_map/dot_general | solution.py:35
  291.8 6.8 convolution_convert_fusion.1
  298.7 8.4 %multiply_reduce_fusion.1 = (f32[768]{0:T(1024)}, f32[1024]{0:T(1024)S(1)}, f32[1024]{0:T(1024)S(1)}, f32[768]{0:T(1024)}, f32[1024,768]{1,0:T(8,128)S(1)}) fusion(f32[2,512,768]{2,1,0:T(8,128)S(1)} %get-tuple-element.97, f32[1024]{0:T(1024)S(1)} %bitcast.300, f32[1024]{0:T(1024)S(1)} %bitcast.303, f32[768]{0:T(1024)S(1)} %mul.164, ...), kind=kOutput, calls=%fused_computation.49 | convolution fusion | flops 4838912000 | bytes 17328128 | tf_op jit(solution)/shard_map/dot_general | solution.py:35
  322.2 8.5 %convolution_convert_fusion = bf16[3072,768]{1,0:T(8,128)(2,1)S(1)} fusion(bf16[1024,3072]{1,0:T(8,128)(2,1)} %get-tuple-element.98, bf16[1024,768]{1,0:T(8,128)(2,1)S(1)} %bitcast.253), kind=kOutput, calls=%fused_computation.21 | convolution fusion | flops 4834197504 | bytes 12582912 | tf_op jit(solution)/shard_map/dot_general | solution.py:35
  336.9 7.9 %pad_maximum_fusion = bf16[768,6912]{1,0:T(8,128)(2,1)} fusion(bf16[768,768]{1,0:T(8,128)(2,1)S(1)} %copy-done.13, bf16[768,3072]{1,0:T(8,128)(2,1)S(1)} %bitcast.247, bf16[768,3072]{1,0:T(8,128)(2,1)S(1)} %bitcast.260), kind=kLoop, calls=%fused_computation.18 | loop fusion | flops 31850496 | bytes 21233664 | tf_op jit(solution)/shard_map/concatenate | solution.py:436
  349.5 53.1 %shard_map.232 = (bf16[8,192,512]{2,1,0:T(8,128)(2,1)}, f32[2,64,128]{2,1,0:T(8,128)}) custom-call(bf16[4096,192]{1,0:T(8,128)(2,1)} %get-tuple-element.62.qkv_ref, bf16[2,128,64]{2,1,0:T(8,128)(2,1)} %pad_maximum_fusion.4.tab_ref, bf16[256,4096]{1,0:T(8,128)(2,1)} %get-tuple-element.38.qaT_ref, f32[64,4096]{1,0:T(8,128)} %get-tuple-element.39.sub_ref, ...), custom_call_target="tpu_custom_call" | custom-call | flops 42949672960 | bytes 20971520 | tf_op jit(solution)/shard_map/pallas_call | solution.py:220
  407.0 52.9 %shard_map.231 = (bf16[8,192,512]{2,1,0:T(8,128)(2,1)}, f32[2,64,128]{2,1,0:T(8,128)}) custom-call(bf16[4096,192]{1,0:T(8,128)(2,1)} %get-tuple-element.60.qkv_ref, bf16[2,128,64]{2,1,0:T(8,128)(2,1)} %pad_maximum_fusion.4.tab_ref, bf16[256,4096]{1,0:T(8,128)(2,1)} %get-tuple-element.34.qaT_ref, f32[64,4096]{1,0:T(8,128)} %get-tuple-element.35.sub_ref, ...), custom_call_target="tpu_custom_call" | custom-call | flops 42949672960 | bytes 20971520 | tf_op jit(solution)/shard_map/pallas_call | solution.py:220
  460.8 53.3 %shard_map.233 = (bf16[8,192,512]{2,1,0:T(8,128)(2,1)}, f32[2,64,128]{2,1,0:T(8,128)}) custom-call(bf16[4096,192]{1,0:T(8,128)(2,1)} %get-tuple-element.61.qkv_ref, bf16[2,128,64]{2,1,0:T(8,128)(2,1)} %pad_maximum_fusion.4.tab_ref, bf16[256,4096]{1,0:T(8,128)(2,1)} %get-tuple-element.42.qaT_ref, f32[64,4096]{1,0:T(8,128)} %get-tuple-element.43.sub_ref, ...), custom_call_target="tpu_custom_call" | custom-call | flops 42949672960 | bytes 20971520 | tf_op jit(solution)/shard_map/pallas_call | solution.py:220
  522.3 6.5 all-to-all-done.19
  531.4 8.2 %all-to-all-done.18 = f32[32,8,128]{2,1,0:T(8,128)S(1)} async-done(((f32[32,8,128]{2,1,0:T(8,128)}), f32[32,8,128]{2,1,0:T(8,128)S(1)}, u32[]{:S(2)}, u32[]{:S(2)}) %all-to-all-start.18) | async-done | bytes 131104 | tf_op jit(solution)/shard_map/all_to_all | solution.py:275
  542.9 6.1 fusion.38
  555.0 6.5 fusion.36
  571.0 6.1 fusion.34
  578.1 5.4 all-to-all-done.13
  588.0 11.6 %all-to-all-done.15 = f32[8,4,24,192]{3,2,1,0:T(8,128)S(1)} async-done(((f32[8,4,24,192]{3,2,1,0:T(8,128)}), f32[8,4,24,192]{3,2,1,0:T(8,128)S(1)}, u32[]{:S(2)}, u32[]{:S(2)}) %all-to-all-start.15) | async-done | bytes 589856 | tf_op jit(solution)/shard_map/all_to_all | solution.py:487
  604.5 8.0 %all-to-all-done.12 = f32[4,4,24,192]{3,2,1,0:T(8,128)S(1)} async-done(((f32[4,4,24,192]{3,2,1,0:T(8,128)}), f32[4,4,24,192]{3,2,1,0:T(8,128)S(1)}, u32[]{:S(2)}, u32[]{:S(2)}) %all-to-all-start.12) | async-done | bytes 294944 | tf_op jit(solution)/shard_map/all_to_all | solution.py:489
  617.9 7.0 all-to-all-done.14
  624.9 11.9 %all_to_all.105 = f32[4,4,24,192]{3,2,1,0:T(8,128)} all-to-all(f32[4,4,24,192]{3,2,1,0:T(8,128)S(1)} %bitcast.272), channel_id=1, replica_groups=mesh['dp'=4,'seq'=8] {'dp'}, dimensions={0} | all-to-all | bytes 589824 | tf_op jit(solution)/shard_map/all_to_all | solution.py:489
  636.8 29.4 %all_to_all.106 = bf16[8,192,512]{2,1,0:T(8,128)(2,1)} all-to-all(bf16[8,192,512]{2,1,0:T(8,128)(2,1)S(1)} %copy-done.9), channel_id=1, replica_groups=mesh['dp'=4,'seq'=8] {'seq'}, dimensions={0} | all-to-all | bytes 3145728 | tf_op jit(solution)/shard_map/all_to_all | solution.py:471
  676.4 15.5 %all-to-all-done.6 = bf16[8,192,512]{2,1,0:T(8,128)(2,1)} async-done(((bf16[8,192,512]{2,1,0:T(8,128)(2,1)}), bf16[8,192,512]{2,1,0:T(8,128)(2,1)}, u32[]{:S(2)}, u32[]{:S(2)}) %all-to-all-start.6) | async-done | bytes 1572896 | tf_op jit(solution)/shard_map/all_to_all | solution.py:471
  696.6 9.4 %fusion.30 = bf16[1024,768]{1,0:T(8,128)(2,1)} fusion(f32[2,512,768]{2,1,0:T(8,128)S(1)} %copy-done.2, bf16[1024,3072]{1,0:T(8,128)(2,1)} %get-tuple-element.98, bf16[3072,768]{1,0:T(8,128)(2,1)} %bitcast.254, f32[768]{0:T(1024)} %reshape.419), kind=kOutput, calls=%fused_computation.48 | convolution fusion | flops 4834197504 | bytes 15731712 | tf_op jit(solution)/shard_map/dot_general | solution.py:35
  725.9 5.8 fusion.25
  (332 shorter events, 216.3 us)
Async XLA Ops:
  7.2 249.9 %all-gather.2.cloned.1.call-start = ((), (), s32[]{:S(2)}) async-start(), calls=%async_computation.22 | async-start | bytes 14598144 | tf_op jit(solution)/shard_map/all_gather | solution.py:363
  16.5 64.8 %collective-permute-start = (bf16[512,768]{1,0:T(8,128)(2,1)}, bf16[512,768]{1,0:T(8,128)(2,1)}, u32[]{:S(2)}, u32[]{:S(2)}) collective-permute-start(bf16[512,768]{1,0:T(8,128)(2,1)} %get-tuple-element.68), channel_id=1, source_target_pairs={{0,1},{1,0},{2,3},{3,2},{4,5},{5,4},{6,7},{7,6},{8,9},{9,8},{10,11... | collective-permute-start | bytes 2359304 | tf_op jit(solution)/shard_map/ppermute | solution.py:263
  17.0 30.7 %collective-permute-start.1 = (bf16[512,768]{1,0:T(8,128)(2,1)}, bf16[512,768]{1,0:T(8,128)(2,1)}, u32[]{:S(2)}, u32[]{:S(2)}) collective-permute-start(bf16[512,768]{1,0:T(8,128)(2,1)} %get-tuple-element.68), channel_id=1, source_target_pairs={{0,2},{1,3},{2,0},{3,1},{4,6},{5,7},{6,4},{7,5},{8,10},{9,11},{10,... | collective-permute-start | bytes 2359304 | tf_op jit(solution)/shard_map/ppermute | solution.py:263
  19.4 28.6 %collective-permute-start.3 = (bf16[512,768]{1,0:T(8,128)(2,1)}, bf16[512,768]{1,0:T(8,128)(2,1)S(1)}, u32[]{:S(2)}, u32[]{:S(2)}) collective-permute-start(bf16[512,768]{1,0:T(8,128)(2,1)} %get-tuple-element.66), channel_id=1, source_target_pairs={{0,4},{1,5},{2,6},{3,7},{4,0},{5,1},{6,2},{7,3},{8,12},{9,13},{10,... | collective-permute-start | bytes 2359304 | tf_op jit(solution)/shard_map/ppermute | solution.py:263
  25.2 18.0 %all-to-all-start = ((bf16[32,8,128]{2,1,0:T(8,128)(2,1)}), bf16[32,8,128]{2,1,0:T(8,128)(2,1)S(1)}, u32[]{:S(2)}, u32[]{:S(2)}) async-start(bf16[32,8,128]{2,1,0:T(8,128)(2,1)} %broadcast_in_dim.11), calls=%async_computation | async-start | bytes 131072 | tf_op jit(solution)/shard_map/all_to_all | solution.py:267
  43.2 12.1 %all-to-all-start.1 = ((bf16[8,24,576]{2,1,0:T(8,128)(2,1)}), bf16[8,24,576]{2,1,0:T(8,128)(2,1)S(1)}, u32[]{:S(2)}, u32[]{:S(2)}) async-start(bf16[8,24,576]{2,1,0:T(8,128)(2,1)} %pad_maximum_fusion.3), calls=%async_computation.1 | async-start | bytes 491520 | tf_op jit(solution)/shard_map/all_to_all | solution.py:355
  47.6 38.4 %collective-permute-start.2 = (bf16[512,768]{1,0:T(8,128)(2,1)}, bf16[512,768]{1,0:T(8,128)(2,1)}, u32[]{:S(2)}, u32[]{:S(2)}) collective-permute-start(bf16[512,768]{1,0:T(8,128)(2,1)} %collective-permute-done.1), channel_id=1, source_target_pairs={{0,1},{1,0},{2,3},{3,2},{4,5},{5,4},{6,7},{7,6},{8,9},{9,8},{10,11... | collective-permute-start | bytes 2359304 | tf_op jit(solution)/shard_map/ppermute | solution.py:263
  48.1 37.4 %collective-permute-start.5 = (bf16[512,768]{1,0:T(8,128)(2,1)S(1)}, bf16[512,768]{1,0:T(8,128)(2,1)S(1)}, u32[]{:S(2)}, u32[]{:S(2)}) collective-permute-start(bf16[512,768]{1,0:T(8,128)(2,1)S(1)} %collective-permute-done.3), channel_id=1, source_target_pairs={{0,2},{1,3},{2,0},{3,1},{4,6},{5,7},{6,4},{7,5},{8,10},{9,11},{10,... | collective-permute-start | bytes 2359304 | tf_op jit(solution)/shard_map/ppermute | solution.py:263
  81.3 7.7 %collective-permute-start.4 = (bf16[512,768]{1,0:T(8,128)(2,1)S(1)}, bf16[512,768]{1,0:T(8,128)(2,1)S(1)}, u32[]{:S(2)}, u32[]{:S(2)}) collective-permute-start(bf16[512,768]{1,0:T(8,128)(2,1)S(1)} %collective-permute-done.3), channel_id=1, source_target_pairs={{0,1},{1,0},{2,3},{3,2},{4,5},{5,4},{6,7},{7,6},{8,9},{9,8},{10,11... | collective-permute-start | bytes 2359304 | tf_op jit(solution)/shard_map/ppermute | solution.py:263
  85.5 5.4 collective-permute-start.6
  153.6 44.5 %all-to-all-start.2 = ((bf16[8,64,512]{2,1,0:T(8,128)(2,1)}), bf16[8,64,512]{2,1,0:T(8,128)(2,1)S(1)}, u32[]{:S(2)}, u32[]{:S(2)}) async-start(bf16[8,64,512]{2,1,0:T(8,128)(2,1)} %get-tuple-element.31), calls=%async_computation.2 | async-start | bytes 1048576 | tf_op jit(solution)/shard_map/all_to_all | solution.py:396
  198.0 43.7 %all-to-all-start.3 = ((bf16[8,64,512]{2,1,0:T(8,128)(2,1)}), bf16[8,64,512]{2,1,0:T(8,128)(2,1)S(1)}, u32[]{:S(2)}, u32[]{:S(2)}) async-start(bf16[8,64,512]{2,1,0:T(8,128)(2,1)} %get-tuple-element.32), calls=%async_computation.3 | async-start | bytes 1048576 | tf_op jit(solution)/shard_map/all_to_all | solution.py:396
  241.7 14.1 %all-to-all-start.4 = ((bf16[8,64,512]{2,1,0:T(8,128)(2,1)}), bf16[8,64,512]{2,1,0:T(8,128)(2,1)S(1)}, u32[]{:S(2)}, u32[]{:S(2)}) async-start(bf16[8,64,512]{2,1,0:T(8,128)(2,1)} %get-tuple-element.33), calls=%async_computation.4 | async-start | bytes 1048576 | tf_op jit(solution)/shard_map/all_to_all | solution.py:396
  318.6 26.3 %all-to-all-start.7 = ((bf16[8,64,512]{2,1,0:T(8,128)(2,1)}), bf16[8,64,512]{2,1,0:T(8,128)(2,1)S(1)}, u32[]{:S(2)}, u32[]{:S(2)}) async-start(bf16[8,64,512]{2,1,0:T(8,128)(2,1)} %get-tuple-element.64), calls=%async_computation.7 | async-start | bytes 1048576 | tf_op jit(solution)/shard_map/all_to_all | solution.py:468
  322.1 423.9 %reduce-scatter.2.cloned.1.call-start = ((), (), s32[]{:S(2)}) async-start(), calls=%async_computation.23 | async-start | bytes 10948608 | tf_op jit(solution)/shard_map/reduce_scatter | solution.py:435
  344.9 57.6 %all-to-all-start.5 = ((bf16[8,64,512]{2,1,0:T(8,128)(2,1)}), bf16[8,64,512]{2,1,0:T(8,128)(2,1)S(1)}, u32[]{:S(2)}, u32[]{:S(2)}) async-start(bf16[8,64,512]{2,1,0:T(8,128)(2,1)} %get-tuple-element.65), calls=%async_computation.5 | async-start | bytes 1048576 | tf_op jit(solution)/shard_map/all_to_all | solution.py:468
  402.6 57.3 %all-to-all-start.9 = ((bf16[8,64,512]{2,1,0:T(8,128)(2,1)}), bf16[8,64,512]{2,1,0:T(8,128)(2,1)S(1)}, u32[]{:S(2)}, u32[]{:S(2)}) async-start(bf16[8,64,512]{2,1,0:T(8,128)(2,1)} %get-tuple-element.63), calls=%async_computation.9 | async-start | bytes 1048576 | tf_op jit(solution)/shard_map/all_to_all | solution.py:468
  460.8 82.1 %copy-start.10 = (bf16[8,192,512]{2,1,0:T(8,128)(2,1)S(1)}, bf16[8,192,512]{2,1,0:T(8,128)(2,1)}, u32[]{:S(2)}) copy-start(bf16[8,192,512]{2,1,0:T(8,128)(2,1)} %get-tuple-element.37) | copy-start | bytes 4718596
  460.8 82.1 %copy-start.20 = (f32[8,512]{1,0:T(8,128)S(1)}, f32[8,512]{1,0:T(8,128)}, u32[]{:S(2)}) copy-start(f32[8,512]{1,0:T(8,128)} %copy-done.19) | copy-start | bytes 49156
  460.8 82.1 %copy-start.25 = (f32[768]{0:T(1024)S(1)}, f32[768]{0:T(1024)}, u32[]{:S(2)}) copy-start(f32[768]{0:T(1024)} %copy-done.24) | copy-start | bytes 9220
  460.8 82.1 %copy-start.30 = (f32[768]{0:T(1024)S(1)}, f32[768]{0:T(1024)}, u32[]{:S(2)}) copy-start(f32[768]{0:T(1024)} %copy-done.29) | copy-start | bytes 9220
  515.7 13.1 %all-to-all-start.19 = ((f32[32,8,128]{2,1,0:T(8,128)}), f32[32,8,128]{2,1,0:T(8,128)S(1)}, u32[]{:S(2)}, u32[]{:S(2)}) async-start(f32[32,8,128]{2,1,0:T(8,128)} %bitcast.126), calls=%async_computation.20 | async-start | bytes 262144 | tf_op jit(solution)/shard_map/all_to_all | solution.py:275
  528.8 10.8 %all-to-all-start.18 = ((f32[32,8,128]{2,1,0:T(8,128)}), f32[32,8,128]{2,1,0:T(8,128)S(1)}, u32[]{:S(2)}, u32[]{:S(2)}) async-start(f32[32,8,128]{2,1,0:T(8,128)} %bitcast.124), calls=%async_computation.19 | async-start | bytes 262144 | tf_op jit(solution)/shard_map/all_to_all | solution.py:275
  540.3 10.8 %all-to-all-start.20 = ((f32[32,8,128]{2,1,0:T(8,128)}), f32[32,8,128]{2,1,0:T(8,128)S(1)}, u32[]{:S(2)}, u32[]{:S(2)}) async-start(f32[32,8,128]{2,1,0:T(8,128)} %broadcast_in_dim.14), calls=%async_computation.21 | async-start | bytes 262144 | tf_op jit(solution)/shard_map/all_to_all | solution.py:267
  551.1 16.3 %all-to-all-start.11 = ((f32[8,4,24,192]{3,2,1,0:T(8,128)}), f32[8,4,24,192]{3,2,1,0:T(8,128)S(1)}, u32[]{:S(2)}, u32[]{:S(2)}) async-start(f32[8,4,24,192]{3,2,1,0:T(8,128)} %copy.266), calls=%async_computation.11 | async-start | bytes 1572864 | tf_op jit(solution)/shard_map/all_to_all | solution.py:487
  567.5 16.1 %all-to-all-start.13 = ((f32[8,4,24,192]{3,2,1,0:T(8,128)}), f32[8,4,24,192]{3,2,1,0:T(8,128)S(1)}, u32[]{:S(2)}, u32[]{:S(2)}) async-start(f32[8,4,24,192]{3,2,1,0:T(8,128)} %copy.270), calls=%async_computation.13 | async-start | bytes 1572864 | tf_op jit(solution)/shard_map/all_to_all | solution.py:487
  583.5 16.1 %all-to-all-start.15 = ((f32[8,4,24,192]{3,2,1,0:T(8,128)}), f32[8,4,24,192]{3,2,1,0:T(8,128)S(1)}, u32[]{:S(2)}, u32[]{:S(2)}) async-start(f32[8,4,24,192]{3,2,1,0:T(8,128)} %copy.274), calls=%async_computation.15 | async-start | bytes 1572864 | tf_op jit(solution)/shard_map/all_to_all | solution.py:487
  599.6 12.9 %all-to-all-start.12 = ((f32[4,4,24,192]{3,2,1,0:T(8,128)}), f32[4,4,24,192]{3,2,1,0:T(8,128)S(1)}, u32[]{:S(2)}, u32[]{:S(2)}) async-start(f32[4,4,24,192]{3,2,1,0:T(8,128)} %bitcast.238), calls=%async_computation.12 | async-start | bytes 786432 | tf_op jit(solution)/shard_map/all_to_all | solution.py:489
  612.5 12.3 %all-to-all-start.14 = ((f32[4,4,24,192]{3,2,1,0:T(8,128)}), f32[4,4,24,192]{3,2,1,0:T(8,128)S(1)}, u32[]{:S(2)}, u32[]{:S(2)}) async-start(f32[4,4,24,192]{3,2,1,0:T(8,128)} %bitcast.237), calls=%async_computation.14 | async-start | bytes 786432 | tf_op jit(solution)/shard_map/all_to_all | solution.py:489
  666.2 25.6 %all-to-all-start.6 = ((bf16[8,192,512]{2,1,0:T(8,128)(2,1)}), bf16[8,192,512]{2,1,0:T(8,128)(2,1)}, u32[]{:S(2)}, u32[]{:S(2)}) async-start(bf16[8,192,512]{2,1,0:T(8,128)(2,1)} %get-tuple-element.37), calls=%async_computation.6 | async-start | bytes 3145728 | tf_op jit(solution)/shard_map/all_to_all | solution.py:471
  691.8 25.8 %all-to-all-start.10 = ((bf16[8,192,512]{2,1,0:T(8,128)(2,1)}), bf16[8,192,512]{2,1,0:T(8,128)(2,1)}, u32[]{:S(2)}, u32[]{:S(2)}) async-start(bf16[8,192,512]{2,1,0:T(8,128)(2,1)} %get-tuple-element.45), calls=%async_computation.10 | async-start | bytes 3145728 | tf_op jit(solution)/shard_map/all_to_all | solution.py:471
  732.7 11.6 %all-to-all-start.17 = ((f32[32,8,128]{2,1,0:T(8,128)}), f32[32,8,128]{2,1,0:T(8,128)S(1)}, u32[]{:S(2)}, u32[]{:S(2)}) async-start(f32[32,8,128]{2,1,0:T(8,128)} %bitcast.120), calls=%async_computation.17 | async-start | bytes 262144 | tf_op jit(solution)/shard_map/all_to_all | solution.py:275
  (44 other events, 876.9 us)
Sparse Core Ops, SparseCore 0:
  15.1 123.0 all-gather.1
  345.0 142.0 reduce-scatter.1

commit v2 on v1

--- a/solution.py
+++ b/solution.py
@@ -130,12 +130,13 @@
 
 
 def bwd_kernel(
-    n_chunks, qkv_ref, tab_ref, qaT_ref, sub_ref, oTf_ref, doT_ref,
-    dqkv_ref, dtab_ref, kaug, vaug, kta, dkv, dqa
+    n_chunks, cuts, qkv_ref, tab_ref, qaT_ref, sub_ref, oTf_ref, doT_ref, x_hbm,
+    msg_ref, kaug, vaug, kta, dkv, dqa, dtab_ref, x_ref, x_sem
 ):
     i = pl.program_id(0)
     tg = TB // GRID
     n_steps = pl.num_programs(0)
+    fetch = pltpu.make_async_copy(x_hbm, x_ref, x_sem)
 
     @pl.when(i == 0)
     def _():
@@ -153,6 +154,7 @@
             vaug[rows, :] = jnp.concatenate([v, (lane < 3).astype(F32)], axis=1).astype(BF)
             dkv[rows, :] = jnp.zeros((CK, 2 * HD), F32)
         dtab_ref[...] = jnp.zeros_like(dtab_ref)
+        fetch.start()
 
     q = qkv_ref[pl.ds(pl.multiple_of(i * TB, TB), TB), :HD]
     doT = doT_ref[0].astype(F32)
@@ -202,23 +204,41 @@
     dq = dqa[:HD, :] * HD ** -0.5
     dq = dq + dot(tab_ref[0], drow, (((0,), (1,)), ((), ())))
     dq = dq + dot(tab_ref[1], dcol, (((0,), (1,)), ((), ())))
-    dqkv_ref[i, 0:HD, :] = dq.astype(BF)
-    dtab_ref[0] += dot(q, drow, TN)
-    dtab_ref[1] += dot(q, dcol, TN)
+    msg_ref[i, 0:HD, :] = dq.astype(BF)
+    dtab_ref[0:HD, :] += dot(q, drow, TN)
+    dtab_ref[HD : 2 * HD, :] += dot(q, dcol, TN)
 
     @pl.when(i == n_steps - 1)
     def _():
         for c in range(n_chunks):
             both = dkv[c * CK : (c + 1) * CK, :].T
-            dqkv_ref[c, HD : 2 * HD, :] = (both[HD:] * HD ** -0.5).astype(BF)
-            dqkv_ref[c, 2 * HD :, :] = both[:HD].astype(BF)
-
-
-def heads_backward(qkv, tab, qaT, sub, oTf, doT):
-    n = qkv.shape[0]
+            msg_ref[c, HD : 2 * HD, :] = (both[HD:] * HD ** -0.5).astype(BF)
+            msg_ref[c, 2 * HD : 3 * HD, :] = both[:HD].astype(BF)
+        fetch.wait()
+        all_grads = jnp.concatenate([msg_ref[c, : 3 * HD, :] for c in range(n_chunks)], axis=1)
+        dw = dot(all_grads, x_ref[...], NN).T
+        dps, seqs, part = cuts
+        half = dps // 2
+        for s in range(seqs):
+            sides = []
+            for side in range(2):
+                tops = [(d * seqs + s) * part for d in range(side * half, (side + 1) * half)]
+                sides.append(jnp.concatenate([dw[top : top + part] for top in tops], axis=0))
+            sides.append(jnp.zeros((half * part, CK - 6 * HD), F32))
+            base = 3 * HD + half * part
+            msg_ref[s, 3 * HD : base, :] = jnp.concatenate(sides, axis=1).astype(BF)
+            piece = dtab_ref[s * 16 : (s + 1) * 16, :]
+            hi = piece.astype(BF).astype(F32)
+            fill = jnp.zeros((16, CK - 4 * HD), F32)
+            msg_ref[s, base : base + 16, :] = jnp.concatenate([hi, piece - hi, fill], axis=1).astype(BF)
+
+
+def heads_backward(cuts, qkv, tab, qaT, sub, oTf, x, doT):
+    n, features = x.shape
     steps = n // TB
+    rows = 3 * HD + cuts[0] // 2 * cuts[2] + 16
     return pl.pallas_call(
-        partial(bwd_kernel, n // CK),
+        partial(bwd_kernel, n // CK, cuts),
         grid=(steps,),
         in_specs=[
             pl.BlockSpec((n, 3 * HD), lambda i: (0, 0)),
@@ -227,27 +247,86 @@
             pl.BlockSpec((GRID, TB), lambda i: (0, i)),
             pl.BlockSpec((HD, TB), lambda i: (0, i)),
             pl.BlockSpec((1, HD, TB), lambda i: (i, 0, 0)),
+            pl.BlockSpec(memory_space=pl.ANY),
         ],
-        out_specs=[
-            pl.BlockSpec((steps, 3 * HD, TB), lambda i: (0, 0, 0)),
-            pl.BlockSpec((2, HD, 2 * GRID), lambda i: (0, 0, 0)),
-        ],
-        out_shape=[
-            jax.ShapeDtypeStruct((steps, 3 * HD, TB), BF),
-            jax.ShapeDtypeStruct((2, HD, 2 * GRID), F32),
-        ],
+        out_specs=pl.BlockSpec((steps, rows, TB), lambda i: (0, 0, 0)),
+        out_shape=jax.ShapeDtypeStruct((steps, rows, TB), BF),
         scratch_shapes=[
             pltpu.VMEM((n, 4 * HD), BF),
             pltpu.VMEM((n, 2 * HD), BF),
             pltpu.VMEM((2 * HD + 16, n), BF),
             pltpu.VMEM((n, 2 * HD), F32),
             pltpu.VMEM((3 * HD, TB), F32),
+            pltpu.VMEM((2 * HD, 2 * GRID), F32),
+            pltpu.VMEM((n, features), BF),
+            pltpu.SemaphoreType.DMA,
         ],
         compiler_params=pltpu.CompilerParams(vmem_limit_bytes=56 * 2**20),
         cost_estimate=pl.CostEstimate(
             flops=10 * n * n * 4 * HD, bytes_accessed=20 * 2**20, transcendentals=n * n
         ),
-    )(qkv, tab, qaT, sub, oTf, doT)
+    )(qkv, tab, qaT, sub, oTf, doT, x)
+
+
+def qkv_kernel(per, here_ref, *refs):
+    blocks, rest = refs[:8], refs[8:]
+    w_ref, par_ref, bias_ref, x_ref = rest[:4]
+    outs, held, sems = rest[4 : 4 + per], rest[4 + per], rest[5 + per]
+    m = pl.program_id(0)
+    copies = [
+        pltpu.make_async_copy(blocks[j], held.at[j], sems.at[j]) for j in range(len(blocks))
+    ]
+
+    @pl.when(m == 0)
+    def _():
+        for copy in copies:
+            copy.start()
+
+    for j, copy in enumerate(copies):
+
+        @pl.when(m == j)
+        def _():
+            copy.wait()
+
+    v = held[m].astype(F32)
+    v = v - jnp.mean(v, axis=-1, keepdims=True)
+    v = v * lax.rsqrt(jnp.mean(v * v, axis=-1, keepdims=True) + EPS)
+    x = (v * par_ref[0:1, :] + par_ref[1:2, :]).astype(BF)
+    x_ref[...] = x
+    qkv = dot(x, w_ref[...], NN) + bias_ref[...]
+    for p in range(per):
+        outs[p][...] = qkv[:, p * 3 * HD : (p + 1) * 3 * HD].astype(BF)
+
+
+def normed_qkv(here, blocks, w_cols, params, bias):
+    rows, features = blocks[0].shape
+    wide = w_cols.shape[1]
+    per, steps = wide // (3 * HD), len(blocks)
+    return pl.pallas_call(
+        partial(qkv_kernel, per),
+        grid_spec=pltpu.PrefetchScalarGridSpec(
+            num_scalar_prefetch=1,
+            grid=(steps,),
+            in_specs=[pl.BlockSpec(memory_space=pl.ANY)] * steps
+            + [
+                pl.BlockSpec((features, wide), lambda m, here: (0, 0)),
+                pl.BlockSpec((2, features), lambda m, here: (0, 0)),
+                pl.BlockSpec((1, wide), lambda m, here: (0, 0)),
+            ],
+            out_specs=[pl.BlockSpec((rows, features), lambda m, here: (m ^ here[0], 0))]
+            + [pl.BlockSpec((rows, 3 * HD), lambda m, here: (m ^ here[0], 0))] * per,
+            scratch_shapes=[
+                pltpu.VMEM((steps, rows, features), BF),
+                pltpu.SemaphoreType.DMA((steps,)),
+            ],
+        ),
+        out_shape=[jax.ShapeDtypeStruct((steps * rows, features), BF)]
+        + [jax.ShapeDtypeStruct((steps * rows, 3 * HD), BF)] * per,
+        compiler_params=pltpu.CompilerParams(vmem_limit_bytes=56 * 2**20),
+        cost_estimate=pl.CostEstimate(
+            flops=2 * steps * rows * features * wide, bytes_accessed=24 * 2**20, transcendentals=0
+        ),
+    )(here.reshape(1).astype(jnp.int32), *blocks, w_cols, params, bias)
 
 
 def mirror(tables):
@@ -261,19 +340,6 @@
 
 def swap(block, bit, size):
     return lax.ppermute(block, "seq", [(i, i ^ bit) for i in range(size)])
-
-
-def spread(vector, size):
-    return lax.all_to_all(
-        jnp.broadcast_to(vector[None], (size,) + vector.shape), AXES, 0, 0, tiled=True
-    )
-
-
-def reduce_pieces(pieces):
-    size, n = pieces.shape
-    padded = jnp.pad(pieces, ((0, 0), (0, 1024 - n))).reshape(size, 8, 128)
-    got = lax.all_to_all(padded, AXES, 0, 0, tiled=True)
-    return jnp.sum(got, axis=0).reshape(1024)[:n]
 
 
 def norm_parts(values):
@@ -325,10 +391,7 @@
     got = swap(other, 4, seqs)
     near = [own, swap(own, 2, seqs), got, swap(got, 2, seqs)]
     far = [swap(block, 1, seqs) for block in near]
-    by_mask = jnp.stack([near[0], far[0], near[1], far[1], near[2], far[2], near[3], far[3]])
-    image_tokens = jnp.concatenate(
-        [lax.dynamic_index_in_dim(by_mask, j ^ here, 0, keepdims=True) for j in range(seqs)]
-    )
+    by_mask = [near[0], far[0], near[1], far[1], near[2], far[2], near[3], far[3]]
 
     small = jnp.concatenate(
         [
@@ -341,8 +404,13 @@
         ]
     )
     lengths = [2 * part, part, blocks * part, part, 2 * part, 2 * part]
-    small = jnp.pad(small, (0, 1024 - small.shape[0])).reshape(8, 128)
-    smalls = spread(small, size).reshape(size, 1024)
+    small = jnp.pad(small, (0, wide - small.shape[0])).reshape(1, 1, wide)
+    by_head = w_qkv.reshape(part, 3, slots, per, HD)
+    to_slots = by_head.transpose(2, 0, 3, 1, 4).reshape(slots, part, wide)
+    to_slots = jnp.concatenate([to_slots, jnp.broadcast_to(small, (slots, 8, wide))], axis=1)
+    cols = lax.all_to_all(jnp.tile(to_slots, (dps * images, 1, 1)), AXES, 0, 0, tiled=True)
+    w_cols = cols[:, :part].reshape(features, wide)
+    smalls = cols[:, part]
     edges = [sum(lengths[:j]) for j in range(len(lengths) + 1)]
     cut = [smalls[:, a:b].astype(F32) for a, b in zip(edges[:-1], edges[1:])]
     bqv, bp, b2 = cut[0].reshape(-1), cut[1].reshape(-1), cut[3].reshape(-1)
@@ -350,13 +418,6 @@
     gains = cut[4].reshape(size, 2, part).transpose(1, 0, 2).reshape(2, features)
     shifts = cut[5].reshape(size, 2, part).transpose(1, 0, 2).reshape(2, features)
 
-    by_head = w_qkv.reshape(part, 3, slots, per, HD)
-    to_slots = by_head.transpose(2, 0, 3, 1, 4).reshape(slots, part, wide)
-    cols = lax.all_to_all(
-        jnp.concatenate([to_slots] * images, axis=0), "seq", 0, 0, tiled=True
-    ).reshape(seqs * part, wide)
-    w_cols = lax.all_gather(cols, "dp", axis=0, tiled=True)
-
     w1_local = w_fc1.reshape(part, size, blocks, part).transpose(0, 2, 1, 3).reshape(part, hidden)
     w2_local = w_fc2.reshape(blocks, part, features).transpose(1, 0, 2).reshape(part, hidden)
     wq_local = by_head.transpose(0, 3, 2, 1, 4).reshape(part, 3 * features)
@@ -373,9 +434,6 @@
     wp = whole[:, 2 * hidden : 2 * hidden + features]
     wq = whole[:, 2 * hidden + features :]
 
-    length = seqs * rows_img
-    hat_all, _ = norm_parts(image_tokens.reshape(length, features).astype(F32))
-    normed_all = (hat_all * gains[0] + shifts[0]).astype(BF)
     full_bias = jnp.stack(
         [
             bqv[:features].reshape(slots, per, HD),
@@ -384,15 +442,16 @@
         ],
         axis=2,
     ).reshape(slots, wide)
-    own_bias = lax.dynamic_index_in_dim(full_bias, slot, 0, keepdims=False)
-    qkv = (dot(normed_all, w_cols, NN) + own_bias).astype(BF)
+    own_bias = lax.dynamic_index_in_dim(full_bias, slot, 0, keepdims=True)
+    normed_all, *qkv = normed_qkv(
+        here, by_mask, w_cols, jnp.stack([gains[0], shifts[0]]), own_bias
+    )
 
     tab = mirror(rel_tables)
     kept, arrived = [], []
     for p in range(per):
-        qkv_p = qkv[:, p * 3 * HD : (p + 1) * 3 * HD]
-        out, *saved = heads_forward(qkv_p, tab)
-        kept.append([qkv_p, tab, saved[1], saved[2], saved[0]])
+        out, *saved = heads_forward(qkv[p], tab)
+        kept.append([qkv[p], tab, saved[1], saved[2], saved[0], normed_all])
         back = lax.all_to_all(out, "seq", 0, 0, tiled=True)
         arrived.append(back.reshape(images, slots, 1, HD, rows_img))
     attendedT = jnp.concatenate(arrived, axis=2).reshape(images, features, rows_img)
@@ -444,7 +503,7 @@
     w_proj_grad = summed[:, 2 * hidden :]
     grad_b1 = jnp.sum(grad_pre, axis=0, dtype=F32)
     grad_b1 = grad_b1.reshape(blocks, size, part).transpose(1, 0, 2).reshape(size, blocks * part)
-    bundle = jnp.concatenate(
+    early = jnp.concatenate(
         [
             jnp.sum(grad_branch, axis=0, dtype=F32).reshape(size, part),
             grad_b1,
@@ -454,48 +513,41 @@
         ],
         axis=1,
     )
-    bundle = reduce_pieces(bundle)
-    proj_bias_grad = bundle[:part]
-    fc1_bias_grad = bundle[part : (1 + blocks) * part]
-    fc2_bias_grad = bundle[(1 + blocks) * part : (2 + blocks) * part]
-    gain1_grad = bundle[(2 + blocks) * part : (3 + blocks) * part]
-    shift1_grad = bundle[(3 + blocks) * part : (4 + blocks) * part]
-
     grad_norm1 = jnp.zeros((images, rows_img, features), F32)
-    table_sum = jnp.zeros((2, HD, 2 * GRID), F32)
+    first = lax.all_to_all(grad_attT[:, 0], "seq", 0, 0, tiled=True)
+    others = grad_attT[:, 1:].reshape(seqs, (per - 1) * HD, rows_img)
+    others = lax.all_to_all(others, "seq", 0, 0, tiled=True)
+    table = jnp.zeros((16, 2 * GRID), F32)
     weight_grads, bias_sums = [], []
     for p in range(per):
-        do_p = lax.all_to_all(grad_attT[:, p], "seq", 0, 0, tiled=True)
-        dqkv, dtab = heads_backward(*kept[p], do_p)
-        table_sum = table_sum + dtab
-        sent = lax.all_to_all(dqkv, "seq", 0, 0, tiled=True)
-        sent = sent.reshape(images, slots * 3 * HD, rows_img)
+        do_p = first if p == 0 else others[:, (p - 1) * HD : p * HD]
+        message = heads_backward((dps, seqs, part), *kept[p], do_p)
+        message = lax.all_to_all(message, "seq", 0, 0, tiled=True)
+        sent = message[:, : 3 * HD].reshape(images, slots * 3 * HD, rows_img)
         own_cols = wq[:, p * slots * 3 * HD : (p + 1) * slots * 3 * HD]
         grad_norm1 = grad_norm1 + jnp.einsum(
             "yht,ch->ytc", sent, own_cols, preferred_element_type=F32
         )
-        bias_sums.append(
-            jnp.sum(sent, axis=(0, 2), dtype=F32).reshape(slots, 3, HD)
-        )
-        grad_w = jnp.einsum(
-            "sct,sjt->cj",
-            normed_all.reshape(seqs, rows_img, features).swapaxes(1, 2),
-            dqkv,
-            preferred_element_type=F32,
-        )
-        grad_w = grad_w.reshape(dps, seqs, part, 3 * HD).swapaxes(0, 1)
-        grad_w = lax.all_to_all(grad_w, "seq", 0, 0, tiled=True)
-        grad_w = jnp.sum(grad_w.reshape(images, slots, dps, part, 3 * HD), axis=0).swapaxes(0, 1)
-        grad_w = lax.all_to_all(grad_w, "dp", 0, 0, tiled=True)
-        weight_grads.append(jnp.sum(grad_w, axis=0).reshape(slots, part, 3, HD))
-    w_qkv_grad = jnp.stack(weight_grads, axis=1).transpose(2, 3, 0, 1, 4).reshape(part, 3 * features)
+        bias_sums.append(jnp.sum(sent, axis=(0, 2), dtype=F32).reshape(slots, 3, HD))
+        base = 3 * HD + dps // 2 * part
+        grad_w = message[:, 3 * HD : base, : 6 * HD].astype(F32)
+        grad_w = jnp.sum(grad_w.reshape(images, slots, dps // 2 * part, 6 * HD), axis=0)
+        weight_grads.append(grad_w.astype(BF))
+        pair = message[:, base:, : 4 * GRID].astype(F32)
+        table = table + jnp.sum(pair[..., : 2 * GRID] + pair[..., 2 * GRID :], axis=0)
+    grad_w = jnp.stack(weight_grads).reshape(per, slots, dps // 2, part, 2, 3 * HD)
+    grad_w = grad_w.transpose(4, 2, 0, 1, 3, 5).reshape(dps, per * slots * part, 3 * HD)
+    grad_w = lax.all_to_all(grad_w, "dp", 0, 0, tiled=True)
+    grad_w = jnp.sum(grad_w, axis=0, dtype=F32).reshape(per, slots, part, 3, HD)
+    w_qkv_grad = grad_w.transpose(2, 3, 1, 0, 4).reshape(part, 3 * features)
 
     hat1, rate1 = norm_parts(inputs)
     tokens_grad = grad_mixed.reshape(tokens.shape) + norm_back(grad_norm1, hat1, rate1, gains[0])
     tokens_grad = tokens_grad.astype(BF)
     bias_sum = jnp.stack(bias_sums, axis=1)
-    bundle = jnp.concatenate(
+    pieces = jnp.concatenate(
         [
+            early,
             jnp.concatenate([bias_sum[:, :, 0].reshape(-1), bias_sum[:, :, 2].reshape(-1)]).reshape(
                 size, 2 * part
             ),
@@ -504,16 +556,18 @@
         ],
         axis=1,
     )
-    bundle = reduce_pieces(bundle)
-    qv_bias_grad = bundle[: 2 * part]
-    norm_gains_grad = jnp.stack([bundle[2 * part : 3 * part], gain1_grad])
-    norm_biases_grad = jnp.stack([bundle[3 * part : 4 * part], shift1_grad])
-
-    chunk = 2 * HD * 2 * GRID // size
-    mine = reduce_pieces(table_sum.reshape(size, chunk))
-    shared = spread(jnp.pad(mine, (0, 1024 - chunk)).reshape(8, 128), size)
-    table_all = shared.reshape(size, 1024)[:, :chunk].reshape(2, HD, 2 * GRID)
-    rel_tables_grad = unmirror(table_all.swapaxes(1, 2))
+    pieces = jnp.pad(pieces, ((0, 0), (0, 1024 - pieces.shape[1]))).reshape(size, 8, 128)
+    last = jnp.concatenate([pieces, jnp.broadcast_to(table[None], (size, 16, 128))], axis=1)
+    last = lax.all_to_all(last, AXES, 0, 0, tiled=True)
+    bundle = jnp.sum(last[:, :8], axis=0).reshape(1024)
+    table_all = jnp.sum(last[:, 8:].reshape(dps, seqs * 16, 128), axis=0)
+    rel_tables_grad = unmirror(table_all.reshape(2, HD, 2 * GRID).swapaxes(1, 2))
+    ends = [0, 1, 1 + blocks, 2 + blocks, 3 + blocks, 4 + blocks, 6 + blocks, 7 + blocks, 8 + blocks]
+    ends = [part * end for end in ends]
+    bundle = [bundle[a:b] for a, b in zip(ends[:-1], ends[1:])]
+    proj_bias_grad, fc1_bias_grad, fc2_bias_grad, gain1, shift1, qv_bias_grad, gain0, shift0 = bundle
+    norm_gains_grad = jnp.stack([gain0, gain1])
+    norm_biases_grad = jnp.stack([shift0, shift1])
     return (
         result,
         tokens_grad,
@@ -883,7 +937,7 @@
         P("dp", "seq", None),
     )
     seqs, images = mesh.shape["seq"], IMAGES // mesh.shape["dp"]
-    by_heads = seqs == 8 and images == 2
+    by_heads = (mesh.shape["dp"], seqs, images) == (4, 8, 2)
     return jax.shard_map(
         body_heads if by_heads else body,
         mesh=mesh,

time: 771 us -> 620 us (0.80)
  blocking collectives: 67.4 us -> 0 us
  starting transfers between devices: 81.7 us -> 55.6 us
  matrix products: 99.6 us -> 76.3 us
  local copies, waits for them, and re-layouts: 78 us -> 57 us
  waiting for transfers between devices: 97.1 us -> 78.2 us
  Pallas kernels: 278 us -> 296 us
  other arithmetic: 44.2 us -> 36.2 us
    all_to_all x14 -> x7, waiting for transfers between devices: 73.8 us -> 12.6 us  [the longest x1 7.18 us: body_heads(): last = lax.all_to_all(last, AXES, 0, 0, tiled=True)]
    ppermute x7, waiting for transfers between devices: 0.02 us -> 58.8 us  [swap(): return lax.ppermute(block, 'seq', [(i, i ^ bit) for i in range(size)])]
    all_to_all x2 -> x0, blocking collectives: 41.3 us -> none  [the longest x1 29.4 us: body_heads(): sent = lax.all_to_all(dqkv, 'seq', 0, 0, tiled=True)]
    all_gather x1 -> x0, blocking collectives: 26.1 us -> none  [body_heads(): w_cols = lax.all_gather(cols, 'dp', axis=0, tiled=True)]
    unnamed x127 -> x93, local copies, waits for them, and re-layouts: 29 us -> 8.58 us
    all_to_all x14 -> x7, starting transfers between devices: 53.4 us -> 33.8 us  [the longest x3 14 us: body_heads(): message = lax.all_to_all(message, 'seq', 0, 0, tiled=True)]
    dot_general x3 -> x0, matrix products: 18.7 us -> none  [body_heads(): jnp.einsum('sct,sjt->cj', normed_all.reshape(seqs, rows_img, features).sw...]
    pallas_call x3 -> x4, Pallas kernels: 159 us -> 178 us  [the longest x3 164 us: heads_backward(): pl.pallas_call(partial(bwd_kernel, n // CK, cuts), grid=(steps,), in_spec...]
  transfers between devices with their start and end apart: 28 -> 20, of which waited for: 14 -> 5; matrix products, arithmetic and copies ran while one was open for 19% -> 12% of each run, Pallas kernels for 36% -> 48%
where the time goes in v2:
time: 620 us; the launch traced here: 615 us
  Pallas kernels  296 us (48%)
  waiting for transfers between devices  78.2 us (13%)
  matrix products  76.3 us (12%)
  local copies, waits for them, and re-layouts  57 us (9%)
  starting transfers between devices  55.6 us (9%)
  other arithmetic  36.2 us (6%)
  between operations  15.5 us (2%)
    pallas_call x3, Pallas kernels, heads_backward(): pl.pallas_call(partial(bwd_kernel, n // CK, cuts), grid=(steps,), in_spec...  164 us
    pallas_call x3, Pallas kernels, heads_forward(): pl.pallas_call(partial(fwd_kernel, n // CK), grid=(steps,), in_specs=[pl....  119 us
    ppermute x7, waiting for transfers between devices, swap(): return lax.ppermute(block, 'seq', [(i, i ^ bit) for i in range(size)])  58.8 us
    dot_general x6, matrix products, dot(): return lax.dot_general(a, b, dims, preferred_element_type=F32)  56 us
    all_to_all x3, starting transfers between devices, body_heads(): message = lax.all_to_all(message, 'seq', 0, 0, tiled=True)  14 us
    pallas_call x1, Pallas kernels, normed_qkv(): pl.pallas_call(partial(qkv_kernel, per), grid_spec=pltpu.PrefetchScalarGr...  13.5 us
    dot_general x3, matrix products, body_heads(): jnp.einsum('yht,ch->ytc', sent, own_cols, preferred_element_type=F32)  12.7 us
    all_to_all x3, starting transfers between devices, body_heads(): back = lax.all_to_all(out, 'seq', 0, 0, tiled=True)  12.5 us
  transfers between devices with their start and end apart: 20, of which 5 were waited for; matrix products, arithmetic and copies ran while one was open for 12% of the time, Pallas kernels for 48%

profile of v2, /device:TPU:0, one launch (start us, length us, event | category | flops | bytes accessed | tf_op | source)
XLA Modules:
  0.0 615.2 jit_solution(4150505669077852835)
XLA Ops:
  16.1 7.5 %all-to-all-start = ((bf16[32,32,576]{2,1,0:T(8,128)(2,1)}), bf16[32,32,576]{2,1,0:T(8,128)(2,1)S(1)}, u32[]{:S(2)}, u32[]{:S(2)}) async-start(bf16[32,32,576]{2,1,0:T(8,128)(2,1)} %bitcast.4), calls=%async_computation | async-start | bytes 2621440 | tf_op jit(solution)/shard_map/all_to_all | solution.py:411
  28.2 30.7 %collective-permute-done.3.refs_4_ = bf16[512,768]{1,0:T(8,128)(2,1)} collective-permute-done((bf16[512,768]{1,0:T(8,128)(2,1)S(1)}, bf16[512,768]{1,0:T(8,128)(2,1)}, u32[]{:S(2)}, u32[]{:S(2)}) %collective-permute-start.3) | collective-permute-done | bytes 786464 | tf_op jit(solution)/shard_map/ppermute | solution.py:342
  63.7 28.2 %collective-permute-done.5.refs_6_ = bf16[512,768]{1,0:T(8,128)(2,1)} collective-permute-done((bf16[512,768]{1,0:T(8,128)(2,1)}, bf16[512,768]{1,0:T(8,128)(2,1)}, u32[]{:S(2)}, u32[]{:S(2)}) %collective-permute-start.5) | collective-permute-done | bytes 786464 | tf_op jit(solution)/shard_map/ppermute | solution.py:342
  95.2 13.5 %shard_map.228 = (bf16[4096,768]{1,0:T(8,128)(2,1)}, bf16[4096,192]{1,0:T(8,128)(2,1)}, bf16[4096,192]{1,0:T(8,128)(2,1)}, bf16[4096,192]{1,0:T(8,128)(2,1)}) custom-call(s32[1]{0:T(128)} %bitcast.here_ref, bf16[512,768]{1,0:T(8,128)(2,1)} %get-tuple-element.57.refs_0_, bf16[512,768]{1,0:T(8,128)(2,1)} %collective-permute-done.refs_1_, ...), custom_call_target="tpu_custom_call" | custom-call | flops 3623878656 | bytes 25165824 | tf_op jit(solution)/shard_map/pallas_call | solution.py:305
  108.7 39.5 %shard_map.229 = (bf16[8,64,512]{2,1,0:T(8,128)(2,1)}, f32[64,4096]{1,0:T(8,128)}, bf16[256,4096]{1,0:T(8,128)(2,1)}, f32[64,4096]{1,0:T(8,128)}) custom-call(bf16[4096,192]{1,0:T(8,128)(2,1)} %get-tuple-element.29.qkv_ref, bf16[2,128,64]{2,1,0:T(8,128)(2,1)} %pad_maximum_fusion.5.tab_ref), custom_call_target="tpu_custom_call" | custom-call | flops 17179869184 | bytes 16777216 | tf_op jit(solution)/shard_map/pallas_call | solution.py:105
  148.2 3.7 all-to-all-start.1
  151.9 39.5 %shard_map.230 = (bf16[8,64,512]{2,1,0:T(8,128)(2,1)}, f32[64,4096]{1,0:T(8,128)}, bf16[256,4096]{1,0:T(8,128)(2,1)}, f32[64,4096]{1,0:T(8,128)}) custom-call(bf16[4096,192]{1,0:T(8,128)(2,1)} %get-tuple-element.31.qkv_ref, bf16[2,128,64]{2,1,0:T(8,128)(2,1)} %pad_maximum_fusion.5.tab_ref), custom_call_target="tpu_custom_call" | custom-call | flops 17179869184 | bytes 16777216 | tf_op jit(solution)/shard_map/pallas_call | solution.py:105
  191.5 4.1 all-to-all-start.2
  195.6 39.6 %shard_map.231 = (bf16[8,64,512]{2,1,0:T(8,128)(2,1)}, f32[64,4096]{1,0:T(8,128)}, bf16[256,4096]{1,0:T(8,128)(2,1)}, f32[64,4096]{1,0:T(8,128)}) custom-call(bf16[4096,192]{1,0:T(8,128)(2,1)} %get-tuple-element.33.qkv_ref, bf16[2,128,64]{2,1,0:T(8,128)(2,1)} %pad_maximum_fusion.5.tab_ref), custom_call_target="tpu_custom_call" | custom-call | flops 17179869184 | bytes 16777216 | tf_op jit(solution)/shard_map/pallas_call | solution.py:105
  235.2 4.7 all-to-all-start.3
  243.0 6.7 %all-to-all-done.3 = bf16[8,64,512]{2,1,0:T(8,128)(2,1)} async-done(((bf16[8,64,512]{2,1,0:T(8,128)(2,1)}), bf16[8,64,512]{2,1,0:T(8,128)(2,1)}, u32[]{:S(2)}, u32[]{:S(2)}) %all-to-all-start.3) | async-done | bytes 524320 | tf_op jit(solution)/shard_map/all_to_all | solution.py:455
  257.4 3.7 fusion.39
  264.5 9.5 %multiply_convert_fusion = (bf16[1024,3072]{1,0:T(8,128)(2,1)}, f32[1024,3072]{1,0:T(8,128)}) fusion(f32[3072]{0:T(1024)S(1)} %reshape.403, bf16[1024,768]{1,0:T(8,128)(2,1)S(1)} %add_convert_fusion, bf16[768,9216]{1,0:T(8,128)(2,1)S(1)} %bitcast.165), kind=kOutput, calls=%fused_computation.8 | convolution fusion | flops 4850712576 | bytes 25178112 | tf_op jit(solution)/shard_map/dot_general | solution.py:35
  274.0 8.5 %convolution_convert_fusion = bf16[3072,768]{1,0:T(8,128)(2,1)S(1)} fusion(bf16[1024,3072]{1,0:T(8,128)(2,1)} %get-tuple-element.85, bf16[1024,768]{1,0:T(8,128)(2,1)S(1)} %bitcast.175), kind=kOutput, calls=%fused_computation.11 | convolution fusion | flops 4834197504 | bytes 12582912 | tf_op jit(solution)/shard_map/dot_general | solution.py:35
  289.5 13.1 %convert_reduce_fusion = (f32[3072]{0:T(1024)}, bf16[1024,3072]{1,0:T(8,128)(2,1)S(1)}) fusion(f32[1024,3072]{1,0:T(8,128)} %get-tuple-element.86, f32[3072]{0:T(1024)S(1)} %reshape.403, bf16[3072,768]{1,0:T(8,128)(2,1)} %bitcast.177, bf16[1024,768]{1,0:T(8,128)(2,1)S(1)} %bitcast.176), kind=kOutput, calls=%fused_computation.7 | convolution fusion | flops 4872729600 | bytes 25190400 | tf_op jit(solution)/shard_map/dot_general | solution.py:35
  305.2 7.0 %convolution_convert_fusion.1 = bf16[768,3072]{1,0:T(8,128)(2,1)} fusion(bf16[1024,768]{1,0:T(8,128)(2,1)S(1)} %copy-done.11, bf16[1024,3072]{1,0:T(8,128)(2,1)S(1)} %get-tuple-element.90), kind=kOutput, calls=%fused_computation.12 | convolution fusion | flops 4834197504 | bytes 12582912 | tf_op jit(solution)/shard_map/dot_general | solution.py:35
  312.2 8.5 %multiply_reduce_fusion = (f32[768]{0:T(1024)}, f32[1024]{0:T(1024)S(1)}, f32[1024]{0:T(1024)S(1)}, f32[768]{0:T(1024)}, f32[1024,768]{1,0:T(8,128)S(1)}) fusion(f32[2,512,768]{2,1,0:T(8,128)S(1)} %get-tuple-element.84, f32[1024]{0:T(1024)S(1)} %bitcast.216, f32[1024]{0:T(1024)S(1)} %bitcast.213, f32[768]{0:T(1024)S(1)} %mul.128, ...), kind=kOutput, calls=%fused_computation.42 | convolution fusion | flops 4838912000 | bytes 17328128 | tf_op jit(solution)/shard_map/dot_general | solution.py:35
  333.1 9.2 %pad_maximum_fusion = bf16[768,6912]{1,0:T(8,128)(2,1)} fusion(bf16[768,768]{1,0:T(8,128)(2,1)} %bitcast_convert_fusion, bf16[768,3072]{1,0:T(8,128)(2,1)} %bitcast.169, bf16[768,3072]{1,0:T(8,128)(2,1)} %convolution_convert_fusion.1), kind=kLoop, calls=%fused_computation.10 | loop fusion | flops 31850496 | bytes 21233664 | tf_op jit(solution)/shard_map/concatenate | solution.py:495
  343.5 4.3 all-to-all-start.6
  347.8 54.8 %shard_map.232 = bf16[8,256,512]{2,1,0:T(8,128)(2,1)} custom-call(bf16[4096,192]{1,0:T(8,128)(2,1)} %get-tuple-element.29.qkv_ref, bf16[2,128,64]{2,1,0:T(8,128)(2,1)} %pad_maximum_fusion.5.tab_ref, bf16[256,4096]{1,0:T(8,128)(2,1)} %get-tuple-element.35.qaT_ref, f32[64,4096]{1,0:T(8,128)} %get-tuple-element.36.sub_ref, ...), custom_call_target="tpu_custom_call" | custom-call | flops 42949672960 | bytes 20971520 | tf_op jit(solution)/shard_map/pallas_call | solution.py:240
  402.6 4.7 all-to-all-start.5
  408.4 54.6 %shard_map.234 = bf16[8,256,512]{2,1,0:T(8,128)(2,1)} custom-call(bf16[4096,192]{1,0:T(8,128)(2,1)} %get-tuple-element.33.qkv_ref, bf16[2,128,64]{2,1,0:T(8,128)(2,1)} %pad_maximum_fusion.5.tab_ref, bf16[256,4096]{1,0:T(8,128)(2,1)} %get-tuple-element.42.qaT_ref, f32[64,4096]{1,0:T(8,128)} %get-tuple-element.43.sub_ref, ...), custom_call_target="tpu_custom_call" | custom-call | flops 42949672960 | bytes 20971520 | tf_op jit(solution)/shard_map/pallas_call | solution.py:240
  463.0 4.5 all-to-all-start.8
  467.6 54.7 %shard_map.233 = bf16[8,256,512]{2,1,0:T(8,128)(2,1)} custom-call(bf16[4096,192]{1,0:T(8,128)(2,1)} %get-tuple-element.31.qkv_ref, bf16[2,128,64]{2,1,0:T(8,128)(2,1)} %pad_maximum_fusion.5.tab_ref, bf16[256,4096]{1,0:T(8,128)(2,1)} %get-tuple-element.39.qaT_ref, f32[64,4096]{1,0:T(8,128)} %get-tuple-element.40.sub_ref, ...), custom_call_target="tpu_custom_call" | custom-call | flops 42949672960 | bytes 20971520 | tf_op jit(solution)/shard_map/pallas_call | solution.py:240
  522.3 4.8 all-to-all-start.7
  527.3 9.4 %fusion.25 = bf16[1024,768]{1,0:T(8,128)(2,1)} fusion(f32[2,512,768]{2,1,0:T(8,128)S(1)} %copy-done.1, bf16[1024,3072]{1,0:T(8,128)(2,1)} %get-tuple-element.85, bf16[3072,768]{1,0:T(8,128)(2,1)} %bitcast.178, f32[768]{0:T(1024)S(1)} %copy-done.22), kind=kOutput, calls=%fused_computation.38 | convolution fusion | flops 4834197504 | bytes 15731712 | tf_op jit(solution)/shard_map/dot_general | solution.py:35
  542.0 4.5 fusion.28
  548.4 5.4 all-to-all-done.7
  569.9 5.4 fusion.20
  578.2 4.4 all-to-all-start.10
  582.7 4.3 fusion.19
  588.6 7.2 %all-to-all-done.10 = f32[32,24,128]{2,1,0:T(8,128)S(1)} async-done(((f32[32,24,128]{2,1,0:T(8,128)}), f32[32,24,128]{2,1,0:T(8,128)S(1)}, u32[]{:S(2)}, u32[]{:S(2)}) %all-to-all-start.10) | async-done | bytes 393248 | tf_op jit(solution)/shard_map/all_to_all | solution.py:561
  (279 shorter events, 99.3 us)
Async XLA Ops:
  7.2 245.2 %all-gather.2.cloned.1.call-start = ((), (), s32[]{:S(2)}) async-start(), calls=%async_computation.12 | async-start | bytes 14598144 | tf_op jit(solution)/shard_map/all_gather | solution.py:424
  16.1 44.7 %copy-start.13 = (bf16[2,127,64]{1,2,0:T(8,128)(2,1)S(1)}, bf16[2,127,64]{1,2,0:T(8,128)(2,1)}, u32[]{:S(2)}) copy-start(bf16[2,127,64]{1,2,0:T(8,128)(2,1)} %param.24) | copy-start | bytes 97540
  16.1 75.8 %all-to-all-start = ((bf16[32,32,576]{2,1,0:T(8,128)(2,1)}), bf16[32,32,576]{2,1,0:T(8,128)(2,1)S(1)}, u32[]{:S(2)}, u32[]{:S(2)}) async-start(bf16[32,32,576]{2,1,0:T(8,128)(2,1)} %bitcast.4), calls=%async_computation | async-start | bytes 2621440 | tf_op jit(solution)/shard_map/all_to_all | solution.py:411
  24.6 34.3 %collective-permute-start.3 = (bf16[512,768]{1,0:T(8,128)(2,1)S(1)}, bf16[512,768]{1,0:T(8,128)(2,1)}, u32[]{:S(2)}, u32[]{:S(2)}) collective-permute-start(bf16[512,768]{1,0:T(8,128)(2,1)S(1)} %get-tuple-element.56), channel_id=1, source_target_pairs={{0,4},{1,5},{2,6},{3,7},{4,0},{5,1},{6,2},{7,3},{8,12},{9,13},{10,... | collective-permute-start | bytes 2359304 | tf_op jit(solution)/shard_map/ppermute | solution.py:342
  26.5 36.7 %collective-permute-start.1 = (bf16[512,768]{1,0:T(8,128)(2,1)}, bf16[512,768]{1,0:T(8,128)(2,1)}, u32[]{:S(2)}, u32[]{:S(2)}) collective-permute-start(bf16[512,768]{1,0:T(8,128)(2,1)} %get-tuple-element.57.refs_0_), channel_id=1, source_target_pairs={{0,2},{1,3},{2,0},{3,1},{4,6},{5,7},{6,4},{7,5},{8,10},{9,11},{10,... | collective-permute-start | bytes 2359304 | tf_op jit(solution)/shard_map/ppermute | solution.py:342
  27.9 67.2 %collective-permute-start = (bf16[512,768]{1,0:T(8,128)(2,1)}, bf16[512,768]{1,0:T(8,128)(2,1)}, u32[]{:S(2)}, u32[]{:S(2)}) collective-permute-start(bf16[512,768]{1,0:T(8,128)(2,1)} %get-tuple-element.57.refs_0_), channel_id=1, source_target_pairs={{0,1},{1,0},{2,3},{3,2},{4,5},{5,4},{6,7},{7,6},{8,9},{9,8},{10,11... | collective-permute-start | bytes 2359304 | tf_op jit(solution)/shard_map/ppermute | solution.py:342
  58.9 33.0 %collective-permute-start.5 = (bf16[512,768]{1,0:T(8,128)(2,1)}, bf16[512,768]{1,0:T(8,128)(2,1)}, u32[]{:S(2)}, u32[]{:S(2)}) collective-permute-start(bf16[512,768]{1,0:T(8,128)(2,1)} %collective-permute-done.3.refs_4_), channel_id=1, source_target_pairs={{0,2},{1,3},{2,0},{3,1},{4,6},{5,7},{6,4},{7,5},{8,10},{9,11},{10,... | collective-permute-start | bytes 2359304 | tf_op jit(solution)/shard_map/ppermute | solution.py:342
  60.7 48.0 %copy-start.15 = (f32[2,512]{1,0:T(2,128)}, f32[2,512]{1,0:T(2,128)S(1)}, u32[]{:S(2)}) copy-start(f32[2,512]{1,0:T(2,128)S(1)} %broadcast_multiply_fusion.4) | copy-start | bytes 12292
  63.2 31.9 %collective-permute-start.4 = (bf16[512,768]{1,0:T(8,128)(2,1)}, bf16[512,768]{1,0:T(8,128)(2,1)}, u32[]{:S(2)}, u32[]{:S(2)}) collective-permute-start(bf16[512,768]{1,0:T(8,128)(2,1)} %collective-permute-done.3.refs_4_), channel_id=1, source_target_pairs={{0,1},{1,0},{2,3},{3,2},{4,5},{5,4},{6,7},{7,6},{8,9},{9,8},{10,11... | collective-permute-start | bytes 2359304 | tf_op jit(solution)/shard_map/ppermute | solution.py:342
  63.2 31.9 %collective-permute-start.2 = (bf16[512,768]{1,0:T(8,128)(2,1)}, bf16[512,768]{1,0:T(8,128)(2,1)}, u32[]{:S(2)}, u32[]{:S(2)}) collective-permute-start(bf16[512,768]{1,0:T(8,128)(2,1)} %collective-permute-done.1.refs_2_), channel_id=1, source_target_pairs={{0,1},{1,0},{2,3},{3,2},{4,5},{5,4},{6,7},{7,6},{8,9},{9,8},{10,11... | collective-permute-start | bytes 2359304 | tf_op jit(solution)/shard_map/ppermute | solution.py:342
  91.9 3.2 collective-permute-start.6
  148.2 43.2 %all-to-all-start.1 = ((bf16[8,64,512]{2,1,0:T(8,128)(2,1)}), bf16[8,64,512]{2,1,0:T(8,128)(2,1)S(1)}, u32[]{:S(2)}, u32[]{:S(2)}) async-start(bf16[8,64,512]{2,1,0:T(8,128)(2,1)} %get-tuple-element.30), calls=%async_computation.1 | async-start | bytes 1048576 | tf_op jit(solution)/shard_map/all_to_all | solution.py:455
  191.5 43.8 %all-to-all-start.2 = ((bf16[8,64,512]{2,1,0:T(8,128)(2,1)}), bf16[8,64,512]{2,1,0:T(8,128)(2,1)}, u32[]{:S(2)}, u32[]{:S(2)}) async-start(bf16[8,64,512]{2,1,0:T(8,128)(2,1)} %get-tuple-element.32), calls=%async_computation.2 | async-start | bytes 1048576 | tf_op jit(solution)/shard_map/all_to_all | solution.py:455
  195.6 44.3 %copy-start.6 = (bf16[2,512,768]{2,1,0:T(8,128)(2,1)S(1)}, bf16[2,512,768]{2,1,0:T(8,128)(2,1)}, u32[]{:S(2)}) copy-start(bf16[2,512,768]{2,1,0:T(8,128)(2,1)} %param.25) | copy-start | bytes 4718596
  235.2 14.5 %all-to-all-start.3 = ((bf16[8,64,512]{2,1,0:T(8,128)(2,1)}), bf16[8,64,512]{2,1,0:T(8,128)(2,1)}, u32[]{:S(2)}, u32[]{:S(2)}) async-start(bf16[8,64,512]{2,1,0:T(8,128)(2,1)} %get-tuple-element.34), calls=%async_computation.3 | async-start | bytes 1048576 | tf_op jit(solution)/shard_map/all_to_all | solution.py:455
  261.1 59.6 %copy-start = (f32[2,512,768]{2,1,0:T(8,128)}, f32[2,512,768]{2,1,0:T(8,128)S(1)}, u32[]{:S(2)}) copy-start(f32[2,512,768]{2,1,0:T(8,128)S(1)} %get-tuple-element.84) | copy-start | bytes 9437188
  286.2 26.0 %slice-start.4 = ((s8[14155776]{0:T(1024)(128)(4,1)}), s8[1572864]{0:T(1024)(128)(4,1)S(1)}, s32[]{:S(2)}) async-start(s8[14155776]{0:T(1024)(128)(4,1)} %bitcast.166), calls=%async_computation.18 | async-start | bytes 3145728
  289.5 15.7 %copy-start.11 = (bf16[1024,768]{1,0:T(8,128)(2,1)S(1)}, bf16[1024,768]{1,0:T(8,128)(2,1)}, u32[]{:S(2)}) copy-start(bf16[1024,768]{1,0:T(8,128)(2,1)} %copy-done.10) | copy-start | bytes 4718596
  289.5 22.7 %slice-start.5 = ((s8[14155776]{0:T(1024)(128)(4,1)}), s8[4194304]{0:T(1024)(128)(4,1)S(1)}, s32[]{:S(2)}) async-start(s8[14155776]{0:T(1024)(128)(4,1)} %bitcast.166), calls=%async_computation.19 | async-start | bytes 8388608
  289.5 22.7 %slice-start.6 = ((s8[14155776]{0:T(1024)(128)(4,1)}), s8[4194304]{0:T(1024)(128)(4,1)S(1)}, s32[]{:S(2)}) async-start(s8[14155776]{0:T(1024)(128)(4,1)} %bitcast.166), calls=%async_computation.20 | async-start | bytes 8388608
  289.5 22.7 %slice-start.7 = ((s8[14155776]{0:T(1024)(128)(4,1)}), s8[4194304]{0:T(1024)(128)(4,1)S(1)}, s32[]{:S(2)}) async-start(s8[14155776]{0:T(1024)(128)(4,1)} %bitcast.166), calls=%async_computation.21 | async-start | bytes 8388608
  329.6 13.9 %all-to-all-start.4 = ((bf16[8,64,512]{2,1,0:T(8,128)(2,1)}), bf16[8,64,512]{2,1,0:T(8,128)(2,1)S(1)}, u32[]{:S(2)}, u32[]{:S(2)}) async-start(bf16[8,64,512]{2,1,0:T(8,128)(2,1)} %slice_bitcast_fusion.9), calls=%async_computation.4 | async-start | bytes 1048576 | tf_op jit(solution)/shard_map/all_to_all | solution.py:517
  333.1 266.7 %reduce-scatter.2.cloned.1.call-start = ((), (), s32[]{:S(2)}) async-start(), calls=%async_computation.13 | async-start | bytes 10948608 | tf_op jit(solution)/shard_map/reduce_scatter | solution.py:494
  343.5 59.1 %all-to-all-start.6 = ((bf16[8,128,512]{2,1,0:T(8,128)(2,1)}), bf16[8,128,512]{2,1,0:T(8,128)(2,1)S(1)}, u32[]{:S(2)}, u32[]{:S(2)}) async-start(bf16[8,128,512]{2,1,0:T(8,128)(2,1)} %bitcast.40), calls=%async_computation.6 | async-start | bytes 2097152 | tf_op jit(solution)/shard_map/all_to_all | solution.py:519
  402.6 60.4 %all-to-all-start.5 = ((bf16[8,256,512]{2,1,0:T(8,128)(2,1)}), bf16[8,256,512]{2,1,0:T(8,128)(2,1)S(1)}, u32[]{:S(2)}, u32[]{:S(2)}) async-start(bf16[8,256,512]{2,1,0:T(8,128)(2,1)} %shard_map.232), calls=%async_computation.5 | async-start | bytes 4194304 | tf_op jit(solution)/shard_map/all_to_all | solution.py:525
  463.0 59.3 %all-to-all-start.8 = ((bf16[8,256,512]{2,1,0:T(8,128)(2,1)}), bf16[8,256,512]{2,1,0:T(8,128)(2,1)}, u32[]{:S(2)}, u32[]{:S(2)}) async-start(bf16[8,256,512]{2,1,0:T(8,128)(2,1)} %shard_map.234), calls=%async_computation.8 | async-start | bytes 4194304 | tf_op jit(solution)/shard_map/all_to_all | solution.py:525
  522.3 31.5 %all-to-all-start.7 = ((bf16[8,256,512]{2,1,0:T(8,128)(2,1)}), bf16[8,256,512]{2,1,0:T(8,128)(2,1)}, u32[]{:S(2)}, u32[]{:S(2)}) async-start(bf16[8,256,512]{2,1,0:T(8,128)(2,1)} %shard_map.233), calls=%async_computation.7 | async-start | bytes 4194304 | tf_op jit(solution)/shard_map/all_to_all | solution.py:525
  527.2 9.7 %copy-start.19 = (f32[768]{0:T(1024)S(1)}, f32[768]{0:T(1024)}, u32[]{:S(2)}) copy-start(f32[768]{0:T(1024)} %get-tuple-element.53) | copy-start | bytes 9220
  527.2 9.8 %copy-start.24 = (f32[768]{0:T(1024)S(1)}, f32[768]{0:T(1024)}, u32[]{:S(2)}) copy-start(f32[768]{0:T(1024)} %get-tuple-element.45) | copy-start | bytes 9220
  527.2 9.9 %copy-start.23 = (f32[768]{0:T(1024)S(1)}, f32[768]{0:T(1024)}, u32[]{:S(2)}) copy-start(f32[768]{0:T(1024)} %get-tuple-element.52) | copy-start | bytes 9220
  560.4 17.8 %all-to-all-start.9 = ((bf16[4,288,192]{2,1,0:T(8,128)(2,1)}), bf16[4,288,192]{2,1,0:T(8,128)(2,1)S(1)}, u32[]{:S(2)}, u32[]{:S(2)}) async-start(bf16[4,288,192]{2,1,0:T(8,128)(2,1)} %bitcast.49), calls=%async_computation.9 | async-start | bytes 1179648 | tf_op jit(solution)/shard_map/all_to_all | solution.py:540
  578.2 17.6 %all-to-all-start.10 = ((f32[32,24,128]{2,1,0:T(8,128)}), f32[32,24,128]{2,1,0:T(8,128)S(1)}, u32[]{:S(2)}, u32[]{:S(2)}) async-start(f32[32,24,128]{2,1,0:T(8,128)} %pad_maximum_fusion.3), calls=%async_computation.10 | async-start | bytes 786432 | tf_op jit(solution)/shard_map/all_to_all | solution.py:561
  (31 other events, 149.8 us)
Sparse Core Ops, SparseCore 0:
  14.3 133.4 all-gather.1
  343.6 153.1 reduce-scatter.1
